TPU v7x, 32 devices: a whole 2x2x4 slice. The times are simulated.
32 devices in a mesh: seq: 8 (over z, y), grp: 4 (over x, core).
Axes of the slice: x: 2, y: 2, z: 4, core: 2. Of those that a mesh axis runs over, the one named last changes fastest.
Arguments:
- tokens_in: bfloat16 [65536, 512], P(('seq', 'grp')), may hold values from -27 to 27, as said below
- seq_starts: int32 [8], replicated, may hold values from 0 to 64511, as said below
- norm_gain: float32 [2, 512], replicated, may hold values from 0.1 to 1.9
- norm_bias: float32 [2, 512], replicated, may hold values from -3 to 3
- decay_rate: float32 [2, 384], replicated, may hold values from 0 to 1, as said below
- step_log: float32 [2, 384], replicated, may hold values from -12 to 0
- frequency: float32 [2, 384], replicated, may hold values from -3 to 3
- in_proj: bfloat16 [2, 512, 768], replicated, may hold values from -0.25 to 0.25
- out_proj: bfloat16 [2, 768, 512], replicated, may hold values from -0.3125 to 0.3125
- skip_gain: float32 [2, 512], replicated, may hold values from -4 to 4
- gate_proj: bfloat16 [2, 512, 512], replicated, may hold values from -0.25 to 0.25
- grad_out: bfloat16 [65536, 512], P(('seq', 'grp')), may hold values from -6 to 6
Outputs:
- layer_out: float32 [65536, 512], P(('seq', 'grp'))
- grad_in: float32 [65536, 512], P(('seq', 'grp'))
- grad_gain: float32 [2, 512], replicated
- grad_bias: float32 [2, 512], replicated
- grad_rate: float32 [2, 384], replicated
- grad_step: float32 [2, 384], replicated
- grad_freq: float32 [2, 384], replicated
- grad_in_proj: float32 [2, 512, 768], replicated
- grad_out_proj: float32 [2, 768, 512], replicated
- grad_skip: float32 [2, 512], replicated
- grad_gate: float32 [2, 512, 512], replicated
Inputs may be any that keep to these rules, and one draw needn't show every extreme that they name: tokens_in drawn in float32 and rounded. `seq_starts`: the first is 0; they increase, consecutive ones differ by more than 1024, and the last lies more than 1024 below 65536. `decay_rate`: positive.
All inputs are finite; a program needn't handle non-finite values.
Results may differ from a plain program's by a relative error of at most 0.02.
Values sent between devices are 32-bit elements; how exact they have to be, the bound alone decides.
No kernel may reach another device: no remote copies, remote signals or barrier semaphores. Data moves between devices by JAX's collectives and lax.ppermute only.
A program may use at most 256 MiB of HBM per device.

v0:
```python
import functools

import jax
import jax.numpy as jnp
from jax import lax
from jax.experimental import pallas as pl
from jax.experimental.pallas import tpu as pltpu
from jax.sharding import Mesh, PartitionSpec as P

LAYERS = 2
EPSILON = 1e-05
SMALL = 8
BLOCKS = 8
SLOT = 4
LANES = 8
VMEM_LIMIT = 30 * 1024 * 1024
GELU_A = 0.7978845608028654
GELU_B = 0.044715
NT = (((1,), (1,)), ((), ()))
TN = (((0,), (0,)), ((), ()))
F32 = jnp.float32
BF16 = jnp.bfloat16


def gather_all(copies, axes):
    return lax.all_to_all(copies, axes, 0, 0)


def scatter_sum(value, axes):
    count = 2 ** len(axes)
    pieces = value.reshape((count, value.shape[0] // count) + value.shape[1:])
    return jnp.sum(lax.all_to_all(pieces, axes, 0, 0), axis=0)


def gather_rows(value, axes):
    count = 2 ** len(axes)
    copies = jnp.broadcast_to(value, (count,) + value.shape)
    return lax.all_to_all(copies, axes, 0, 0).reshape((count * value.shape[0],) + value.shape[1:])


def phases(axes):
    left, out = list(axes), [(axes[-1],)]
    left = left[:-1]
    while left:
        out.append(tuple(left[-2:]))
        left = left[:-2]
    return out


def sum_all(value, parts):
    for part in parts:
        value = scatter_sum(value, part)
    for part in reversed(parts):
        value = gather_rows(value, part)
    return value


def cols(c):
    return slice(c * 128, (c + 1) * 128)


def chunk_count(ref):
    return ref.shape[-1] // 256


def rows_of(ref, at, chunks):
    half = chunks * 128
    re = [ref[at, c * 128 : (c + 1) * 128] for c in range(chunks)]
    im = [ref[at, half + c * 128 : half + (c + 1) * 128] for c in range(chunks)]
    return re, im


def put_rows(ref, at, re, im):
    chunks = len(re)
    half = chunks * 128
    for c in range(chunks):
        ref[at, c * 128 : (c + 1) * 128] = re[c]
        ref[at, half + c * 128 : half + (c + 1) * 128] = im[c]


def put_copies(ref, re, im):
    ref[0] = jnp.zeros(ref.shape[1:], F32)
    for c in range(len(re)):
        ref[0, c : c + 1] = re[c]
        ref[0, SLOT + c : SLOT + c + 1] = im[c]
    ref[...] = jnp.broadcast_to(ref[0:1], ref.shape)


def wide(rows):
    return [jnp.broadcast_to(v, (LANES, 128)) for v in rows]


def chain(ends_ref, jr_ref, power, carry, down, start_ref=None):
    chunks = len(power[0])
    pr, pi = power
    cr, ci = carry
    order = range(LANES - 1, -1, -1) if down else range(LANES)
    for s in order:
        at = slice(s, s + 1)
        if start_ref is not None:
            put_rows(start_ref, at, cr, ci)
        er, ei = rows_of(ends_ref, at, chunks)
        alive = (jr_ref[at, :] < 0).astype(F32)
        cr, ci = (
            [er[c] + alive * (pr[c] * cr[c] - pi[c] * ci[c]) for c in range(chunks)],
            [ei[c] + alive * (pr[c] * ci[c] + pi[c] * cr[c]) for c in range(chunks)],
        )
    return cr, ci


def carry_in(ends_ref, table_ref, chunks):
    total = jnp.zeros((2 * SLOT, 128), F32)
    for e in range(ends_ref.shape[0]):
        end = ends_ref[e]
        turned = jnp.concatenate([end[SLOT:], end[:SLOT]], axis=0)
        total += table_ref[0, e] * end + table_ref[1, e] * turned
    return (
        [total[c : c + 1] for c in range(chunks)],
        [total[SLOT + c : SLOT + c + 1] for c in range(chunks)],
    )


def in_stages(stages, parts):
    for turn in range(len(parts) + len(stages) - 1):
        for k, stage in enumerate(stages):
            if 0 <= turn - k < len(parts):
                stage(parts[turn - k])


def parts_of(rows, down):
    half = rows // 2 if rows >= 32 * LANES else rows
    parts = [(at, at + half) for at in range(0, rows, half)]
    return parts[::-1] if down else parts


class Scan:
    def __init__(self, src_ref, st_ref, decay, jr_ref, first_step, down):
        self.src_ref, self.st_ref, self.down = src_ref, st_ref, down
        self.chunks = chunk_count(src_ref)
        self.dr, self.di = wide(decay[0]), wide(decay[1])
        self.jr, self.first_step = jr_ref[...], first_step
        self.state = rows_of(st_ref, slice(0, LANES), self.chunks)

    def one(self, step):
        br, bi = rows_of(self.src_ref, slice(step * LANES, (step + 1) * LANES), self.chunks)
        live = self.jr != self.first_step + step
        nr, ni = [], []
        for c in range(self.chunks):
            xr = jnp.where(live, self.state[0][c], 0.0)
            xi = jnp.where(live, self.state[1][c], 0.0)
            nr.append(self.dr[c] * xr - self.di[c] * xi + br[c])
            ni.append(self.dr[c] * xi + self.di[c] * xr + bi[c])
        self.state = (nr, ni)
        return nr, ni

    def run(self, part, emit=None):
        low, high = part[0] // LANES, part[1] // LANES
        for n in range(0, high - low, 2):
            step = high - 2 - n if self.down else low + n
            first = self.one(step + 1 if self.down else step)
            second = self.one(step if self.down else step + 1)
            if emit is not None:
                pair = (second, first) if self.down else (first, second)
                emit(slice(step * LANES, (step + 2) * LANES), pair)

    def close(self):
        put_rows(self.st_ref, slice(0, LANES), *self.state)


def store_pair(ref, at, first, second):
    re = [jnp.concatenate([p, q], axis=0).astype(BF16) for p, q in zip(first[0], second[0])]
    im = [jnp.concatenate([p, q], axis=0).astype(BF16) for p, q in zip(first[1], second[1])]
    put_rows(ref, at, re, im)


def disc_row(disc_ref, row, chunks, conj=False):
    re, im = rows_of(disc_ref, slice(row, row + 1), chunks)
    return (re, [-v for v in im]) if conj else (re, im)


def column_sum(value):
    rows, width = value.shape
    return jnp.sum(jnp.sum(value.reshape(rows // 8, 8, width), axis=0), axis=0, keepdims=True)


def permute_in(block_ref, order_ref, part):
    runs, _, width = block_ref.shape
    size = order_ref.shape[0]
    span = size // runs
    out = []
    for k in range(part[0] // size, part[1] // size):
        rows = block_ref[:, k * span : (k + 1) * span, :].reshape(size, width)
        out.append(jnp.dot(order_ref[...], rows, preferred_element_type=F32))
    return out[0] if len(out) == 1 else jnp.concatenate(out, axis=0)


def permute_out(value, order_ref, out_ref, part):
    width = value.shape[1]
    size = order_ref.shape[0]
    span = size // LANES
    high = value.astype(BF16)
    low = (value - high.astype(F32)).astype(BF16)
    for n, k in enumerate(range(part[0] // size, part[1] // size)):
        at = slice(n * size, (n + 1) * size)
        back = lax.dot_general(order_ref[...], high[at], TN, preferred_element_type=F32)
        back += lax.dot_general(order_ref[...], low[at], TN, preferred_element_type=F32)
        out_ref[:, k * span : (k + 1) * span, :] = back.reshape(LANES, span, width)


def expm1(value):
    acc = jnp.full_like(value, 1.0 / 479001600.0)
    for n in (39916800.0, 3628800.0, 362880.0, 40320.0, 5040.0, 720.0, 120.0, 24.0, 6.0, 2.0, 1.0):
        acc = acc * value + 1.0 / n
    return jnp.where(value > -1.0, acc * value, jnp.exp(value) - 1.0)


def prep_kernel(
    rows, axes, starts_ref, rate_ref, step_ref, freq_ref,
    disc_ref, table_ref, cut_ref, order_ref,
):
    devices = 2 ** len(axes)
    total = rows * devices
    run = rows // LANES
    half = rate_ref.shape[-1]
    me = 0
    for axis in axes:
        me = 2 * me + lax.axis_index(axis)
    starts = [starts_ref[:, k : k + 1] for k in range(starts_ref.shape[1])]

    base = me * rows + run * lax.broadcasted_iota(jnp.int32, (LANES, 128), 0)
    up = jnp.full((LANES, 128), -1, jnp.int32)
    down = up
    for begin in starts + [total]:
        rel = begin - base
        up = jnp.maximum(up, jnp.where((rel >= 0) & (rel < run), rel, -1))
        down = jnp.maximum(down, jnp.where((rel >= 1) & (rel <= run), rel - 1, -1))
    cut_ref[0] = up
    cut_ref[1] = down

    size = order_ref.shape[0]
    span = size // LANES
    to = lax.broadcasted_iota(jnp.int32, (size, size), 0)
    back = lax.broadcasted_iota(jnp.int32, (size, size), 1)
    order_ref[...] = ((to % LANES) * span + to // LANES == back).astype(F32).astype(BF16)

    source = lax.broadcasted_iota(jnp.int32, (devices, half), 0)
    for l in range(LAYERS):
        row = slice(l, l + 1)
        rate, freq = rate_ref[row], freq_ref[row]
        step_size = jnp.exp(step_ref[row])
        real_angle = -rate * step_size
        imag_angle = freq * step_size
        magnitude = jnp.exp(real_angle)
        cosine, sine = jnp.cos(imag_angle), jnp.sin(imag_angle)
        minus_real = expm1(real_angle) * cosine - 2.0 * jnp.sin(0.5 * imag_angle) ** 2
        minus_imag = magnitude * sine
        modulus = rate * rate + freq * freq
        disc_ref[l, 0:1, :half] = magnitude * cosine
        disc_ref[l, 0:1, half:] = minus_imag
        disc_ref[l, 1:2, :half] = (-rate * minus_real + freq * minus_imag) / modulus
        disc_ref[l, 1:2, half:] = (-rate * minus_imag - freq * minus_real) / modulus
        magnitude = jnp.exp(real_angle * float(run))
        disc_ref[l, 2:3, :half] = magnitude * jnp.cos(imag_angle * float(run))
        disc_ref[l, 2:3, half:] = magnitude * jnp.sin(imag_angle * float(run))
        disc_ref[l, 3:8] = jnp.zeros((5, 2 * half), F32)
        powers = []
        for bit in range(len(axes)):
            magnitude = jnp.exp(real_angle * float(rows << bit))
            angle = imag_angle * float(rows << bit)
            powers.append((magnitude * jnp.cos(angle), magnitude * jnp.sin(angle)))
        for back in range(2):
            going_down = (l + back) % 2 == 1
            if going_down:
                live, count = source > me, source - me - 1
            else:
                live, count = source < me, me - 1 - source
            for begin in starts:
                if going_down:
                    cut = (begin > (me + 1) * rows) & (source * rows >= begin)
                else:
                    cut = (begin < me * rows) & ((source + 1) * rows <= begin)
                live &= ~cut
            count = jnp.maximum(count, 0)
            real = live.astype(F32)
            imag = jnp.zeros((devices, half), F32)
            for bit, (pr, pi) in enumerate(powers):
                use = (count & (1 << bit)) != 0
                pr, pi = jnp.where(use, pr, 1.0), jnp.where(use, pi, 0.0)
                real, imag = real * pr - imag * pi, real * pi + imag * pr
            imag = -imag if back else imag
            at = 2 * l + back
            table_ref[at] = jnp.zeros(table_ref.shape[1:], F32)
            for c in range(half // 128):
                table_ref[at, 0, :, c, :] = real[:, cols(c)]
                table_ref[at, 0, :, SLOT + c, :] = real[:, cols(c)]
                table_ref[at, 1, :, c, :] = -imag[:, cols(c)]
                table_ref[at, 1, :, SLOT + c, :] = imag[:, cols(c)]


def stats_kernel(tok_ref, order_ref, u_ref, copy_ref, stats_ref):
    value = permute_in(tok_ref, order_ref, (0, u_ref.shape[0]))
    u_ref[...] = value.astype(BF16)
    copy_ref[...] = u_ref[...]
    zero_first(stats_ref)
    add_stats(stats_ref, value)
    spread_last(stats_ref)


def add_stats(stats_ref, value):
    add_rows(stats_ref, column_sum(value), column_sum(value * value))


def add_rows(copies_ref, first, second):
    for c in range(first.shape[1] // 128):
        copies_ref[0, c : c + 1] += first[:, cols(c)]
        copies_ref[0, SLOT + c : SLOT + c + 1] += second[:, cols(c)]


def summed(ref):
    total = jnp.sum(ref[...], axis=0)
    return tuple(
        jnp.concatenate([total[SLOT * k + c : SLOT * k + c + 1] for c in range(SLOT)], axis=1)
        for k in range(2)
    )


def drive_kernel(layer, down, tokens, *refs):
    (
        stat_ref, u_ref, gain_ref, bias_ref, skip_ref, win_ref, disc_ref, jr_ref,
        b_ref, end_ref, blk_ref, norm_ref,
    ) = refs
    i, nt = pl.program_id(0), pl.num_programs(0)
    steps = u_ref.shape[0] // LANES
    chunks = chunk_count(b_ref)
    half = chunks * 128

    @pl.when(i == 0)
    def _():
        total, squares = summed(stat_ref)
        row = slice(layer, layer + 1)
        mean = total / tokens
        inv = lax.rsqrt(squares / tokens - mean * mean + EPSILON)
        norm_ref[0:1] = mean
        norm_ref[1:2] = inv
        norm_ref[2:3] = inv * gain_ref[row]
        norm_ref[3:4] = bias_ref[row]
        norm_ref[4:5] = skip_ref[row]
        norm_ref[5:8] = jnp.zeros((3, norm_ref.shape[1]), F32)
        blk_ref[...] = jnp.zeros_like(blk_ref)

    fr, fi = disc_ref[1:2, :half], disc_ref[1:2, half:]
    tile = nt - 1 - i if down else i
    scan = Scan(b_ref, blk_ref, disc_row(disc_ref, 0, chunks), jr_ref, tile * steps, down)

    def product(part):
        at = slice(*part)
        u = u_ref[at].astype(F32)
        normed = (u - norm_ref[0:1]) * norm_ref[2:3] + norm_ref[3:4]
        drive = jnp.dot(normed.astype(BF16), win_ref[...], preferred_element_type=F32)
        re, im = drive[:, :half], drive[:, half:]
        b_ref[at, :half] = re * fr - im * fi
        b_ref[at, half:] = re * fi + im * fr

    in_stages([product, scan.run], parts_of(b_ref.shape[0], down))
    scan.close()

    @pl.when(i == nt - 1)
    def _():
        zero = [jnp.zeros((1, 128), F32)] * chunks
        cr, ci = chain(blk_ref, jr_ref, disc_row(disc_ref, 2, chunks), (zero, zero), down)
        put_copies(end_ref, cr, ci)


def states_scan(ends_ref, table_ref, b_ref, blk_ref, disc_ref, jr_ref, low_ref, st_ref, down):
    i, nt = pl.program_id(0), pl.num_programs(0)
    chunks = chunk_count(b_ref)
    steps = b_ref.shape[0] // LANES

    @pl.when(i == 0)
    def _():
        carry = carry_in(ends_ref, table_ref, chunks)
        chain(blk_ref, jr_ref, disc_row(disc_ref, 2, chunks), carry, down, st_ref)

    tile = nt - 1 - i if down else i
    scan = Scan(b_ref, st_ref, disc_row(disc_ref, 0, chunks), jr_ref, tile * steps, down)

    def stage(part):
        scan.run(part, lambda at, pair: store_pair(low_ref, at, *pair))

    return scan, stage


def gelu_parts(mixed):
    square = mixed * mixed
    tanh = jnp.tanh(mixed * (GELU_A + (GELU_A * GELU_B) * square))
    half_up = 0.5 + 0.5 * tanh
    return square, tanh, half_up


def gelu_slope(mixed, square, tanh, half_up):
    return half_up + (mixed * (0.5 - 0.5 * tanh * tanh)) * (
        GELU_A + (3.0 * GELU_A * GELU_B) * square
    )


def sigmoid(value):
    return 0.5 + 0.5 * jnp.tanh(0.5 * value)


def forward_kernel(down, *refs):
    (
        ends_ref, table_ref, b_ref, blk_ref, disc_ref, jr_ref, u_ref, norm_ref, wout_ref, wgate_ref,
        next_ref, copy_ref, low_ref, mixed_ref, gate_ref, stats_ref, st_ref,
    ) = refs
    scan, states = states_scan(
        ends_ref, table_ref, b_ref, blk_ref, disc_ref, jr_ref, low_ref, st_ref, down
    )
    zero_first(stats_ref)
    acts = {}

    def mix(part):
        at = slice(*part)
        u = u_ref[at].astype(F32)
        normed = (u - norm_ref[0:1]) * norm_ref[2:3] + norm_ref[3:4]
        mixed = jnp.dot(low_ref[at], wout_ref[...], preferred_element_type=F32)
        mixed += norm_ref[4:5] * normed
        _, _, half_up = gelu_parts(mixed)
        acts[part] = mixed * half_up
        mixed_ref[at] = mixed.astype(BF16)

    def finish(part):
        at = slice(*part)
        act = acts[part]
        gate = sigmoid(jnp.dot(act.astype(BF16), wgate_ref[...], preferred_element_type=F32))
        after = u_ref[at].astype(F32) + act * gate
        next_ref[at] = after
        copy_ref[at] = after
        gate_ref[at] = gate.astype(BF16)
        add_stats(stats_ref, after)

    in_stages([states, mix, finish], parts_of(b_ref.shape[0], down))
    scan.close()
    spread_last(stats_ref)


def zero_first(*refs):
    @pl.when(pl.program_id(0) == 0)
    def _():
        for ref in refs:
            ref[...] = jnp.zeros(ref.shape, ref.dtype)


def spread_last(ref):
    @pl.when(pl.program_id(0) == pl.num_programs(0) - 1)
    def _():
        ref[...] = jnp.broadcast_to(ref[0:1], ref.shape)


class GateBackward:
    def __init__(self, low_ref, wout_ref, wgate_ref, pg_ref, sg_ref, wsum_ref, ssum_ref, acts):
        self.low_ref, self.wout_ref, self.wgate_ref = low_ref, wout_ref, wgate_ref
        self.pg_ref, self.sg_ref = pg_ref, sg_ref
        self.wsum_ref, self.ssum_ref = wsum_ref, ssum_ref
        self.act_ref, self.logit_ref = acts
        self.kept = {}

    def enter(self, part, g, mixed, gate, normed, kept=None):
        at = slice(*part)
        square, tanh, half_up = gelu_parts(mixed) if kept is None else kept
        act = mixed * half_up
        g_gate = g * gate
        if kept is None:
            self.act_ref[at] = act.astype(BF16)
        self.logit_ref[at] = (g_gate * act * (1.0 - gate)).astype(BF16)
        self.kept[part] = (g_gate, gelu_slope(mixed, square, tanh, half_up), normed)

    def middle(self, part):
        at = slice(*part)
        g_gate, slope, normed = self.kept[part]
        act_grad = g_gate + lax.dot_general(
            self.logit_ref[at], self.wgate_ref[...], NT, preferred_element_type=F32
        )
        mixed_grad = act_grad * slope
        self.ssum_ref[...] += column_sum(mixed_grad * normed)
        self.pg_ref[at] = mixed_grad.astype(BF16)

    def leave(self, part):
        at = slice(*part)
        self.sg_ref[at] = lax.dot_general(
            self.pg_ref[at], self.wout_ref[...], NT, preferred_element_type=F32
        )

    def sums(self):
        states, width = self.wout_ref.shape
        self.wsum_ref[states : states + width] += lax.dot_general(
            self.act_ref[...], self.logit_ref[...], TN, preferred_element_type=F32
        )
        self.wsum_ref[:states] += lax.dot_general(
            self.low_ref[...], self.pg_ref[...], TN, preferred_element_type=F32
        )


def turn_kernel(down, *refs):
    (
        ends_ref, table_ref, b_ref, blk_ref, disc_ref, jr_ref, jo_ref, u_ref, norm_ref, wout_ref, wgate_ref,
        gout_ref, order_ref,
        out_ref, low_ref, g_ref, pg_ref, sg_ref, wsum_ref, end_ref, ablk_ref,
        st_ref, w_ref, act_ref, logit_ref,
    ) = refs
    sums = wout_ref.shape[0] + wout_ref.shape[1]
    ssum_ref = wsum_ref.at[sums : sums + 1]
    i, nt = pl.program_id(0), pl.num_programs(0)
    chunks = chunk_count(b_ref)
    half = chunks * 128
    steps = b_ref.shape[0] // LANES
    tile = nt - 1 - i if down else i
    scan, states = states_scan(
        ends_ref, table_ref, b_ref, blk_ref, disc_ref, jr_ref, low_ref, st_ref, down
    )
    back = GateBackward(
        low_ref, wout_ref, wgate_ref, pg_ref, sg_ref, wsum_ref, ssum_ref, (act_ref, logit_ref)
    )

    @pl.when(i == 0)
    def _():
        wsum_ref[...] = jnp.zeros(wsum_ref.shape, F32)
        ablk_ref[...] = jnp.zeros(ablk_ref.shape, F32)
        w_ref[:, :half] = jnp.ones((LANES, half), F32)
        w_ref[:, half:] = jnp.zeros((LANES, half), F32)

    mid = {}

    def mix(part):
        at = slice(*part)
        u = u_ref[at]
        normed = (u - norm_ref[0:1]) * norm_ref[2:3] + norm_ref[3:4]
        mixed = jnp.dot(low_ref[at], wout_ref[...], preferred_element_type=F32)
        mixed += norm_ref[4:5] * normed
        kept = gelu_parts(mixed)
        act_ref[at] = (mixed * kept[2]).astype(BF16)
        mid[part] = (normed, mixed, kept)

    def enter(part):
        at = slice(*part)
        normed, mixed, kept = mid[part]
        gate = sigmoid(jnp.dot(act_ref[at], wgate_ref[...], preferred_element_type=F32))
        permute_out(u_ref[at] + (mixed * kept[2]) * gate, order_ref, out_ref, part)
        g = permute_in(gout_ref, order_ref, part)
        g_ref[at] = g.astype(BF16)
        back.enter(part, g, mixed, gate, normed, kept)

    dr, di = disc_row(disc_ref, 0, chunks, conj=True)
    dr, di = wide(dr), wide(di)
    jo = jo_ref[...]
    live = {
        "w": rows_of(w_ref, slice(0, LANES), chunks),
        "a": rows_of(ablk_ref, slice(0, LANES), chunks),
    }

    def weigh(part):
        (wr, wi), (ar, ai) = (tuple(map(list, live[k])) for k in "wa")
        order = range(part[0] // LANES, part[1] // LANES)
        for step in reversed(order) if down else order:
            sr, si = rows_of(sg_ref, slice(step * LANES, (step + 1) * LANES), chunks)
            keep = jo != tile * steps + step
            for c in range(chunks):
                ar[c] = ar[c] + (wr[c] * sr[c] - wi[c] * si[c])
                ai[c] = ai[c] + (wr[c] * si[c] + wi[c] * sr[c])
                xr = jnp.where(keep, wr[c], 0.0)
                xi = jnp.where(keep, wi[c], 0.0)
                wr[c] = xr * dr[c] - xi * di[c]
                wi[c] = xr * di[c] + xi * dr[c]
        live["w"], live["a"] = (wr, wi), (ar, ai)

    in_stages(
        [states, mix, enter, back.middle, back.leave, weigh], parts_of(b_ref.shape[0], down)
    )
    back.sums()
    scan.close()
    put_rows(w_ref, slice(0, LANES), *live["w"])
    put_rows(ablk_ref, slice(0, LANES), *live["a"])

    @pl.when(i == nt - 1)
    def _():
        zero = [jnp.zeros((1, 128), F32)] * chunks
        power = disc_row(disc_ref, 2, chunks, conj=True)
        cr, ci = chain(ablk_ref, jo_ref, power, (zero, zero), not down)
        put_copies(end_ref, cr, ci)


def adjoint_kernel(down, last, *refs):
    (
        ends_ref, table_ref, sg_ref, ablk_ref, disc_ref, jr_ref, low_ref, u_ref, norm_ref, pg_ref, g_ref,
        win_ref, order_ref, *refs
    ) = refs
    if last:
        (
            ssum_ref, res_ref, sums_ref, st_ref, dg_ref, ax_ref, low_normed_ref, nsum_ref, isum_ref,
        ) = refs
    else:
        (res_ref, sums_ref, nsum_ref, st_ref, dg_ref, ax_ref, low_normed_ref) = refs
        isum_ref = sums_ref
    width, states = win_ref.shape
    i, nt = pl.program_id(0), pl.num_programs(0)
    chunks = chunk_count(sg_ref)
    half = chunks * 128
    steps = sg_ref.shape[0] // LANES
    tile = nt - 1 - i if down else i

    @pl.when(i == 0)
    def _():
        carry = carry_in(ends_ref, table_ref, chunks)
        power = disc_row(disc_ref, 2, chunks, conj=True)
        chain(ablk_ref, jr_ref, power, carry, down, st_ref)
        ax_ref[...] = jnp.zeros_like(ax_ref)

    zero_first(isum_ref, nsum_ref)
    fr, fi = disc_row(disc_ref, 1, chunks)
    fr, fi = wide(fr), wide(fi)
    decay = disc_row(disc_ref, 0, chunks, conj=True)
    scan = Scan(sg_ref, st_ref, decay, jr_ref, tile * steps, down)
    sums = tuple(map(list, rows_of(ax_ref, slice(0, LANES), chunks)))

    def emit(at, pair):
        xr, xi = rows_of(low_ref, at, chunks)
        xr, xi = [v.astype(F32) for v in xr], [v.astype(F32) for v in xi]
        grads = []
        for which, (ar, ai) in enumerate(pair):
            gr, gi = [], []
            rows = slice(which * LANES, (which + 1) * LANES)
            for c in range(chunks):
                vr, vi = xr[c][rows], xi[c][rows]
                sums[0][c] = sums[0][c] + (ar[c] * vr + ai[c] * vi)
                sums[1][c] = sums[1][c] + (ai[c] * vr - ar[c] * vi)
                gr.append(ar[c] * fr[c] + ai[c] * fi[c])
                gi.append(ai[c] * fr[c] - ar[c] * fi[c])
            grads.append((gr, gi))
        store_pair(dg_ref, at, *grads)

    def finish(part):
        at = slice(*part)
        centered = u_ref[at].astype(F32) - norm_ref[0:1]
        low_normed_ref[at] = (centered * norm_ref[2:3] + norm_ref[3:4]).astype(BF16)
        normed_grad = lax.dot_general(dg_ref[at], win_ref[...], NT, preferred_element_type=F32)
        normed_grad += norm_ref[4:5] * pg_ref[at].astype(F32)
        add_rows(
            nsum_ref, column_sum(normed_grad), column_sum(normed_grad * centered) * norm_ref[1:2]
        )
        result = g_ref[at].astype(F32) + norm_ref[2:3] * normed_grad
        if last:
            permute_out(result, order_ref, res_ref, part)
        else:
            res_ref[at] = result

    in_stages([lambda part: scan.run(part, emit), finish], parts_of(sg_ref.shape[0], down))
    isum_ref[:width] += lax.dot_general(
        low_normed_ref[...], dg_ref[...], TN, preferred_element_type=F32
    )
    scan.close()
    put_rows(ax_ref, slice(0, LANES), *sums)
    spread_last(nsum_ref)

    @pl.when(i == nt - 1)
    def _():
        decays = jnp.sum(ax_ref[...], axis=0, keepdims=True)
        wr, wi = win_ref[:, :half].astype(F32), win_ref[:, half:].astype(F32)
        gr, gi = isum_ref[:width, :half], isum_ref[:width, half:]
        re = jnp.sum(wr * gr + wi * gi, axis=0, keepdims=True)
        im = jnp.sum(wr * gi - wi * gr, axis=0, keepdims=True)
        gr, gi = disc_ref[1:2, :half], disc_ref[1:2, half:]
        scale = 1.0 / (gr * gr + gi * gi)
        factors = ((re * gr - im * gi) * scale, (re * gi + im * gr) * scale)
        if last:
            rows = width // BLOCKS
            first = rows + rows // 2
            for b in range(BLOCKS):
                at = b * rows
                sums_ref[b, :rows] = isum_ref[at : at + rows, :width]
                sums_ref[b, rows:first, : states - width] = isum_ref[at : at + rows // 2, width:]
                sums_ref[b, rows:first, states - width :] = isum_ref[
                    at + rows // 2 : at + rows, width:
                ]
                sums_ref[b, first:] = jnp.zeros((SMALL, width), F32)
            small = [nsum_ref[0]] + [ssum_ref[:, cols(c)] for c in range(width // 128)]
            small += [decays[:, cols(c)] for c in range(2 * chunks)]
            small += [v[:, cols(c)] for v in factors for c in range(chunks)]
            small = [v[r : r + 1] for v in small for r in range(v.shape[0])]
            for k, row in enumerate(small):
                at = (k % SMALL, k // SMALL)
                sums_ref[0, first + at[0] : first + at[0] + 1, cols(at[1])] = row
        else:
            sums_ref[width : width + 1] = decays
            sums_ref[width + 1 : width + 2, :half] = factors[0]
            sums_ref[width + 1 : width + 2, half:] = factors[1]


def back_kernel(down, tokens, core, *refs):
    (
        sums_ref, r_ref, up_ref, up_norm_ref, mixed_ref, gate_ref, low_ref, u_ref, norm_ref, wout_ref,
        wgate_ref, disc_ref, jo_ref,
        g_ref, pg_ref, sg_ref, kept_ref, sent_ref, ssum_ref, end_ref, ablk_ref, nsum_ref, bsum_ref, wsum_ref,
        act_ref, logit_ref,
    ) = refs
    i, nt = pl.program_id(0), pl.num_programs(0)
    chunks = chunk_count(sg_ref)
    steps = sg_ref.shape[0] // LANES
    tile = nt - 1 - i if down else i

    @pl.when(i == 0)
    def _():
        nsum_ref[...] = jnp.sum(sums_ref[...], axis=0)
        bsum_ref[0:1], bsum_ref[1:2] = summed(sums_ref)

    zero_first(ablk_ref, wsum_ref, ssum_ref)
    back = GateBackward(
        low_ref, wout_ref, wgate_ref, pg_ref, sg_ref, wsum_ref, ssum_ref, (act_ref, logit_ref)
    )
    decay = disc_row(disc_ref, 0, chunks, conj=True)
    scan = Scan(sg_ref, ablk_ref, decay, jo_ref, tile * steps, down)
    scale = up_norm_ref[2:3] * (-1.0 / tokens)

    def enter(part):
        at = slice(*part)
        standard = (up_ref[at] - up_norm_ref[0:1]) * (scale * up_norm_ref[1:2] * bsum_ref[1:2])
        g = r_ref[at] + (standard + scale * bsum_ref[0:1])
        g_ref[at] = g
        u = u_ref[at].astype(F32)
        normed = (u - norm_ref[0:1]) * norm_ref[2:3] + norm_ref[3:4]
        back.enter(part, g, mixed_ref[at].astype(F32), gate_ref[at].astype(F32), normed)

    in_stages([enter, back.middle, back.leave, scan.run], parts_of(sg_ref.shape[0], down))
    back.sums()
    scan.close()

    @pl.when(i == nt - 1)
    def _():
        zero = [jnp.zeros((1, 128), F32)] * chunks
        power = disc_row(disc_ref, 2, chunks, conj=True)
        cr, ci = chain(ablk_ref, jo_ref, power, (zero, zero), down)
        put_copies(end_ref, cr, ci)
        states, width = wout_ref.shape
        gates, outs = width // BLOCKS, states // BLOCKS
        side = lax.axis_index(core)
        for ref, first in ((kept_ref, side), (sent_ref, 1 - side)):
            for b in range(BLOCKS // 2):
                at = first * (BLOCKS // 2) + b
                ref[b, :gates] = wsum_ref[pl.ds(pl.multiple_of(states + at * gates, 8), gates)]
                ref[b, gates:] = wsum_ref[pl.ds(pl.multiple_of(at * outs, 8), outs)]


def last_kernel(
    tokens, piece_ref, small_ref, out1_ref, gate1_ref, skip1_ref, in1_ref, decay1_ref, norm1_ref,
    disc_ref, rate_ref, step_ref, freq_ref, r_ref, tok_ref, norm_ref,
    grad_in_ref, gain_ref, bias_ref, drate_ref, dstep_ref, dfreq_ref, in_ref, out_ref, skip_ref,
    gate_ref,
):
    gates, width = gate1_ref.shape
    outs = out1_ref.shape[0]
    states = in1_ref.shape[1]
    half = states // 2
    left = states - width
    gate_ref[0], gate_ref[1] = piece_ref[:gates], gate1_ref[...]
    out_ref[0], out_ref[1] = piece_ref[gates : gates + outs], out1_ref[...]
    at = gates + outs
    in_ref[0, :, :width] = piece_ref[at : at + gates]
    at += gates
    in_ref[0, : gates // 2, width:] = piece_ref[at : at + gates // 2, :left]
    in_ref[0, gates // 2 :, width:] = piece_ref[at : at + gates // 2, left:]
    in_ref[1] = in1_ref[...]

    def row(ref, first, count):
        places = [(k % SMALL, k // SMALL) for k in range(first, first + count)]
        return jnp.concatenate([ref[r : r + 1, cols(c)] for r, c in places], axis=1)

    count = width // 128
    bias, gain = row(small_ref, 0, count), row(small_ref, count, count)
    scale = norm_ref[2:3] * (-1.0 / tokens)
    grad_in_ref[...] = r_ref[...] + (
        (tok_ref[...].astype(F32) - norm_ref[0:1]) * (scale * norm_ref[1:2] * gain) + scale * bias
    )

    @pl.when(pl.program_id(0) == 0)
    def _():
        bias_ref[0:1], gain_ref[0:1] = bias, gain
        bias_ref[1:2], gain_ref[1:2] = row(norm1_ref, 0, count), row(norm1_ref, count, count)
        skip_ref[0:1], skip_ref[1:2] = row(small_ref, 2 * count, count), skip1_ref[0:1]
        at = 3 * count
        lanes = half // 128
        for l in range(LAYERS):
            if l == 0:
                ar, ai, sr, si = (row(small_ref, at + k * lanes, lanes) for k in range(4))
            else:
                ar, ai = decay1_ref[0:1, :half], decay1_ref[0:1, half:]
                sr, si = decay1_ref[1:2, :half], decay1_ref[1:2, half:]
            dr, di = disc_ref[l, 0:1, :half], disc_ref[l, 0:1, half:]
            fr, fi = disc_ref[l, 1:2, :half], disc_ref[l, 1:2, half:]
            here = slice(l, l + 1)
            rate, freq, step = rate_ref[here], freq_ref[here], jnp.exp(step_ref[here])
            tr = ar - (fr * sr + fi * si)
            ti = ai - (fr * si - fi * sr)
            size = 1.0 / (dr * dr + di * di)
            gr, gi = (tr * dr - ti * di) * size, (tr * di + ti * dr) * size
            mr, mi = -rate * fr - freq * fi, freq * fr - rate * fi
            size = 1.0 / (rate * rate + freq * freq)
            gr += (-rate * sr - freq * si) * size
            gi += (freq * sr - rate * si) * size
            both = 2.0 * (fr * sr + fi * si)
            gx = gr * dr + gi * di
            gy = gi * dr - gr * di
            drate_ref[here] = (-mr * sr - mi * si - both * rate) * size - step * gx
            dfreq_ref[here] = (mi * sr - mr * si - both * freq) * size + step * gy
            dstep_ref[here] = step * (freq * gy - rate * gx)


def whole(array):
    shape = array.shape
    return pl.BlockSpec(shape, lambda i: (0,) * len(shape))


def tile_spec(rows, width, nt, down):
    if down:
        return pl.BlockSpec((rows, width), lambda i: (nt - 1 - i, 0))
    return pl.BlockSpec((rows, width), lambda i: (i, 0))


def run_spec(steps, width, nt, down):
    if down:
        return pl.BlockSpec((LANES, steps, width), lambda i: (0, nt - 1 - i, 0))
    return pl.BlockSpec((LANES, steps, width), lambda i: (0, i, 0))


def call(kernel, nt, args, outs, scratch, macs, name):
    arrays = [a for a, *_ in args]
    sizes = sum(a.size * a.dtype.itemsize for a in arrays + [a for a, *_ in outs])
    held = [
        a if keep is None else pltpu.with_memory_space_constraint(a, keep)
        for a, _, keep in map(filled, args)
    ]
    return pl.pallas_call(
        kernel,
        grid=(nt,),
        in_specs=[whole(a) if s is None else s for a, s, _ in map(filled, args)],
        out_specs=[whole(a) if s is None else s for a, s, _ in map(filled, outs)],
        out_shape=[
            a if keep is None else keep(a.shape, a.dtype) for a, _, keep in map(filled, outs)
        ],
        scratch_shapes=scratch,
        compiler_params=pltpu.CompilerParams(
            vmem_limit_bytes=VMEM_LIMIT, dimension_semantics=("arbitrary",)
        ),
        cost_estimate=pl.CostEstimate(flops=2 * macs, bytes_accessed=sizes, transcendentals=0),
        name=name,
    )(*held)


def filled(entry):
    return entry if len(entry) == 3 else entry + (pltpu.HBM,)


def shape(*dims, dtype=F32):
    return jax.ShapeDtypeStruct(dims, dtype)


def body(
    axes,
    tokens_in,
    seq_starts,
    norm_gain,
    norm_bias,
    decay_rate,
    step_log,
    frequency,
    in_proj,
    out_proj,
    skip_gain,
    gate_proj,
    grad_out,
):
    rows, width = tokens_in.shape
    states = in_proj.shape[-1]
    devices = 2 ** len(axes)
    tokens = float(rows * devices)
    run = rows // LANES
    steps = min(64, run)
    tile = steps * LANES
    nt = rows // tile
    span = min(32, steps)
    def tiles(array, down):
        return (array, tile_spec(tile, array.shape[-1], nt, down))

    def runs(array, down):
        return (array, run_spec(steps, array.shape[-1], nt, down))

    def full(array):
        return (array, None)

    def of(array, l):
        size = array.shape[1:]
        return (array, pl.BlockSpec((None,) + size, lambda i: (l,) + (0,) * len(size)))

    discs, tables, cuts, order = call(
        functools.partial(prep_kernel, rows, axes), 1,
        [full(seq_starts[None]), full(decay_rate),
         full(step_log), full(frequency)],
        [full(shape(LAYERS, 8, states)), full(shape(2 * LAYERS, 2, devices, 2 * SLOT, 128)),
         full(shape(2, LANES, 128, dtype=jnp.int32)),
         full(shape(span * LANES, span * LANES, dtype=BF16))],
        [], rows * width, "prep",
    )

    def near(entry):
        return entry[:2] + (pltpu.VMEM if rows * states * 4 <= 7 * 2**20 else pltpu.HBM,)

    tokens_run = tokens_in.reshape(LANES, run, width)
    grad_run = grad_out.reshape(LANES, run, width)
    state_scratch = pltpu.VMEM((LANES, states), F32)
    half_scratch = [pltpu.VMEM((tile, width), BF16)] * 2
    cost = rows * width * states

    u0_near, u0, stats = call(
        stats_kernel, nt, [runs(tokens_run, 0), full(order)],
        [near(tiles(shape(rows, width, dtype=BF16), 0)), tiles(shape(rows, width, dtype=BF16), 0),
         near(full(shape(devices, 2 * SLOT, 128)))],
        [], cost // 2, "stats",
    )

    def drive(l, stream, stats):
        down = l % 2
        return call(
            functools.partial(drive_kernel, l, bool(down), tokens), nt,
            [near(full(gather_all(stats, axes))), near(tiles(stream, down)), full(norm_gain), full(norm_bias), full(skip_gain), of(in_proj, l), of(discs, l),
               of(cuts, down)],
            [near(tiles(shape(rows, states), down)), near(full(shape(devices, 2 * SLOT, 128))),
             full(shape(LANES, states)), full(shape(8, width))],
            [], 4 * cost, f"drive_{l}",
        )

    b0, end0, blk0, norm0 = drive(0, u0_near, stats)
    u1_near, u1, low0, mixed0, gate0, stats = call(
        functools.partial(forward_kernel, False), nt,
        [near(full(gather_all(end0, axes))), of(tables, 2 * 0 + 0), near(tiles(b0, 0)), full(blk0), of(discs, 0), of(cuts, 0),
           near(tiles(u0_near, 0)), full(norm0), of(out_proj, 0), of(gate_proj, 0)],
        [near(tiles(shape(rows, width), 0)), tiles(shape(rows, width), 0), tiles(shape(rows, states, dtype=BF16), 0),
         tiles(shape(rows, width, dtype=BF16), 0), tiles(shape(rows, width, dtype=BF16), 0),
         near(full(shape(devices, 2 * SLOT, 128)))],
        [state_scratch], 6 * cost, "forward_0",
    )

    b1, end1, blk1, norm1 = drive(1, u1_near, stats)
    (
        out, low1, g1, pg1, sg1, w_sum1, aend1, ablk1
    ) = call(
        functools.partial(turn_kernel, True), nt,
        [near(full(gather_all(end1, axes))), of(tables, 2 * 1 + 0), near(tiles(b1, 1)), full(blk1), of(discs, 1), of(cuts, 1),
           of(cuts, 0), tiles(u1, 1), full(norm1), of(out_proj, 1), of(gate_proj, 1),
           runs(grad_run, 1), full(order)],
        [runs(shape(LANES, run, width), 1), near(tiles(shape(rows, states, dtype=BF16), 1)),
         near(tiles(shape(rows, width, dtype=BF16), 1)),
         near(tiles(shape(rows, width, dtype=BF16), 1)), near(tiles(shape(rows, states), 1)), full(shape(states + width + 8, width)),
         near(full(shape(devices, 2 * SLOT, 128))), full(shape(LANES, states))],
        [state_scratch, state_scratch] + half_scratch, 16 * cost, "turn_1",
    )

    def adjoint(l, sg, ablk, ends, low, stream, norm, pg, g, skip_sum=None):
        down = 1 - l % 2
        last = l == 0
        held = (lambda entry: entry) if last else near
        args = [
            near(full(ends)), of(tables, 2 * l + 1), held(tiles(sg, down)), full(ablk), of(discs, l),
            of(cuts, down), held(tiles(low, down)), tiles(stream, down),
            full(norm), held(tiles(pg, down)), held(tiles(g, down)), of(in_proj, l), full(order),
        ]
        scratch = [
            state_scratch, pltpu.VMEM((tile, states), BF16), state_scratch,
            pltpu.VMEM((tile, width), BF16),
        ]
        if last:
            args.append(full(skip_sum))
            outs = [
                runs(shape(LANES, run, width), down),
                full(shape(BLOCKS, (width + width // 2) // BLOCKS + SMALL, width)),
            ]
            scratch += [pltpu.VMEM((1, 2 * SLOT, 128), F32), pltpu.VMEM((width, states), F32)]
        else:
            outs = [
                tiles(shape(rows, width), down), full(shape(width + 8, states)),
                near(full(shape(devices, 2 * SLOT, 128))),
            ]
        return call(
            functools.partial(adjoint_kernel, bool(down), last), nt, args, outs, scratch,
            8 * cost, f"adjoint_{l}",
        )

    r1, in_sum1, norm_sum1 = adjoint(
        1, sg1, ablk1, gather_all(aend1, axes), low1, u1, norm1, pg1, g1
    )

    piece = (2 * width + states + width // 2) // BLOCKS + SMALL

    def lower(r1, norm_sum1):
        half = shape(BLOCKS // 2, (states + width) // BLOCKS, width)
        (
            g0, pg0, sg0, kept0, sent0, skip_sum0, aend0, ablk0, small1, _
        ) = call(
            functools.partial(back_kernel, True, tokens, axes[-1]), nt,
            [near(full(gather_all(norm_sum1, axes))), tiles(r1, 1), tiles(u1, 1), full(norm1),
             tiles(mixed0, 1), tiles(gate0, 1), tiles(low0, 1), tiles(u0, 1), full(norm0),
             of(out_proj, 0), of(gate_proj, 0), of(discs, 0), of(cuts, 1)],
            [tiles(shape(rows, width), 1), tiles(shape(rows, width, dtype=BF16), 1),
             tiles(shape(rows, states), 1), full(half), full(half), full(shape(1, width)), near(full(shape(devices, 2 * SLOT, 128))),
             full(shape(LANES, states)), full(shape(2 * SLOT, 128)), full(shape(2, width))],
            [pltpu.VMEM((states + width, width), F32)] + half_scratch, 12 * cost, "back_0",
        )
        core, chips, *others = phases(axes)
        part = kept0 + lax.ppermute(sent0, core[0], [(0, 1), (1, 0)])
        ends, part = lax.optimization_barrier((gather_all(aend0, axes), part))
        part = part.reshape(-1, width)
        part = scatter_sum(part, chips)
        r0, in_sum0 = adjoint(0, sg0, ablk0, ends, low0, u0, norm0, pg0, g0, skip_sum0)
        in_sum0, part = lax.optimization_barrier((in_sum0, part))
        in_part = scatter_sum(scatter_sum(in_sum0.reshape(-1, width), core), chips)
        pad = -piece % (8 * 2 ** len(others[0]))
        part = jnp.concatenate([part, in_part, jnp.zeros((pad, width), F32)], axis=0)
        part = sum_all(part, others)[:piece]
        pieces = gather_rows(gather_rows(part, chips), core)
        return r0.reshape(rows, width), small1, pieces.reshape(BLOCKS, -1, width)

    def nothing(r1, norm_sum1):
        return (
            jnp.zeros((rows, width), F32),
            jnp.zeros((2 * SLOT, 128), F32),
            jnp.zeros((BLOCKS, piece, width), F32),
        )

    w_all1, in_all1 = lax.psum((w_sum1, in_sum1), axes)
    r0, norm_all1, pieces = lax.cond(seq_starts[0] == 0, lower, nothing, r1, norm_sum1)

    gates, outs = width // BLOCKS, states // BLOCKS

    def block(array, *dims, at=lambda i: (i, 0)):
        return (array, pl.BlockSpec(dims, at))

    def flat(array, count):
        return block(array, count, array.shape[1])

    (
        grad_in, gain_grad, bias_grad, rate_grad, step_grad, freq_grad, in_grad, out_grad,
        skip_grad, gate_grad,
    ) = call(
        functools.partial(last_kernel, tokens), BLOCKS,
        [block(pieces, None, piece, width, at=lambda i: (i, 0, 0)) + (None,),
         block(pieces, None, SMALL, width, at=lambda i: (0, piece // SMALL - 1, 0)) + (None,),
         flat(w_all1, outs),
         block(w_all1, gates, width, at=lambda i: (states // gates + i, 0)),
         block(w_all1, 8, width, at=lambda i: ((states + width) // 8, 0)),
         flat(in_all1, gates),
         block(in_all1, 8, states, at=lambda i: (width // 8, 0)),
         full(norm_all1), full(discs), full(decay_rate), full(step_log), full(frequency),
         flat(r0, rows // BLOCKS), flat(tokens_in, rows // BLOCKS), full(norm0)],
        [flat(shape(rows, width), rows // BLOCKS), full(shape(LAYERS, width)),
         full(shape(LAYERS, width)), full(shape(LAYERS, states // 2)),
         full(shape(LAYERS, states // 2)), full(shape(LAYERS, states // 2)),
         block(shape(LAYERS, width, states), LAYERS, gates, states, at=lambda i: (0, i, 0)),
         block(shape(LAYERS, states, width), LAYERS, outs, width, at=lambda i: (0, i, 0)),
         full(shape(LAYERS, width)),
         block(shape(LAYERS, width, width), LAYERS, gates, width, at=lambda i: (0, i, 0))],
        [], cost, "last",
    )
    return (
        out.reshape(rows, width),
        grad_in,
        gain_grad,
        bias_grad,
        rate_grad,
        step_grad,
        freq_grad,
        in_grad,
        out_grad,
        skip_grad,
        gate_grad,
    )


def solution(mesh):
    bits = mesh.devices.size.bit_length() - 1
    axes = tuple("b%d" % k for k in range(bits))
    binary = Mesh(mesh.devices.reshape((2,) * bits), axes)
    rows = P(axes, None)
    return jax.shard_map(
        functools.partial(body, axes),
        mesh=binary,
        in_specs=(rows,) + (P(),) * 10 + (rows,),
        out_specs=(rows, rows) + (P(),) * 9,
        check_vma=False,
    )
```

profile of v0, /device:TPU:0, one launch (start us, length us, event | category | flops | bytes accessed | tf_op | source)
XLA Modules:
  0.0 308.1 jit_solution(16708189922464400330)
XLA Ops:
  10.0 4.7 %stats.1 = (bf16[2048,512]{1,0:T(8,128)(2,1)S(1)}, bf16[2048,512]{1,0:T(8,128)(2,1)}, f32[32,8,128]{2,1,0:T(8,128)S(1)}) custom-call(bf16[8,256,512]{2,1,0:T(8,128)(2,1)} %bitcast.16, bf16[256,256]{1,0:T(8,128)(2,1)} %get-tuple-element.119.order_ref.refs_12_), custom_call_target="tpu_custom_call" | custom-call | flops 805306368 | bytes 6553600 | tf_op jit(solution)/shard_map/stats/pallas_call | solution.py:839
  14.7 15.3 %all_to_all.67.refs_0_ = f32[32,8,128]{2,1,0:T(8,128)S(1)} all-to-all(f32[32,8,128]{2,1,0:T(8,128)S(1)} %get-tuple-element.120), channel_id=1, replica_groups=mesh['b0'=2,'b1'=2,'b2'=2,'b3'=2,'b4'=2] {'b0','b1','b2','b3','b4'}, dimensions={0} | all-to-all | bytes 262144 | tf_op jit(solution)/shard_map/all_to_all | solution.py:26
  30.0 4.9 %drive_0.1 = (f32[2048,768]{1,0:T(8,128)S(1)}, f32[32,8,128]{2,1,0:T(8,128)S(1)}, f32[8,768]{1,0:T(8,128)}, f32[8,512]{1,0:T(8,128)}) custom-call(f32[32,8,128]{2,1,0:T(8,128)S(1)} %all_to_all.67.refs_0_, bf16[2048,512]{1,0:T(8,128)(2,1)S(1)} %get-tuple-element.121.refs_1_.refs_6_, f32[2,512]{1,0:T(2,128)} %refs_2_.3, f32[2,512]{1,0:T(2,128)} %refs_3_.3, ...), custom_call_target="tpu_custom_call" | custom-call | flops 6442450944 | bytes 10334208 | tf_op jit(solution)/shard_map/drive_0/pallas_call | solution.py:839
  34.9 10.0 %all_to_all.68.refs_0_ = f32[32,8,128]{2,1,0:T(8,128)S(1)} all-to-all(f32[32,8,128]{2,1,0:T(8,128)S(1)} %get-tuple-element.124), channel_id=1, replica_groups=mesh['b0'=2,'b1'=2,'b2'=2,'b3'=2,'b4'=2] {'b0','b1','b2','b3','b4'}, dimensions={0} | all-to-all | bytes 262144 | tf_op jit(solution)/shard_map/all_to_all | solution.py:26
  44.9 9.2 %forward_0.1 = (f32[2048,512]{1,0:T(8,128)S(1)}, f32[2048,512]{1,0:T(8,128)}, bf16[2048,768]{1,0:T(8,128)(2,1)}, bf16[2048,512]{1,0:T(8,128)(2,1)}, bf16[2048,51...) custom-call(f32[32,8,128]{2,1,0:T(8,128)S(1)} %all_to_all.68.refs_0_, f32[4,2,32,8,128]{4,3,2,1,0:T(8,128)} %get-tuple-element.125.refs_1_, ...), custom_call_target="tpu_custom_call" | custom-call | flops 9663676416 | bytes 28147712 | tf_op jit(solution)/shard_map/forward_0/pallas_call | solution.py:839
  54.1 10.0 %all_to_all.69.refs_0_ = f32[32,8,128]{2,1,0:T(8,128)S(1)} all-to-all(f32[32,8,128]{2,1,0:T(8,128)S(1)} %get-tuple-element.129), channel_id=1, replica_groups=mesh['b0'=2,'b1'=2,'b2'=2,'b3'=2,'b4'=2] {'b0','b1','b2','b3','b4'}, dimensions={0} | all-to-all | bytes 262144 | tf_op jit(solution)/shard_map/all_to_all | solution.py:26
  64.1 5.3 %drive_1.1 = (f32[2048,768]{1,0:T(8,128)S(1)}, f32[32,8,128]{2,1,0:T(8,128)S(1)}, f32[8,768]{1,0:T(8,128)}, f32[8,512]{1,0:T(8,128)}) custom-call(f32[32,8,128]{2,1,0:T(8,128)S(1)} %all_to_all.69.refs_0_, f32[2048,512]{1,0:T(8,128)S(1)} %get-tuple-element.130.refs_1_, f32[2,512]{1,0:T(2,128)} %refs_2_.3, f32[2,512]{1,0:T(2,128)} %refs_3_.3, ...), custom_call_target="tpu_custom_call" | custom-call | flops 6442450944 | bytes 12431360 | tf_op jit(solution)/shard_map/drive_1/pallas_call | solution.py:839
  69.4 10.0 %all_to_all.70.refs_0_ = f32[32,8,128]{2,1,0:T(8,128)S(1)} all-to-all(f32[32,8,128]{2,1,0:T(8,128)S(1)} %get-tuple-element.131), channel_id=1, replica_groups=mesh['b0'=2,'b1'=2,'b2'=2,'b3'=2,'b4'=2] {'b0','b1','b2','b3','b4'}, dimensions={0} | all-to-all | bytes 262144 | tf_op jit(solution)/shard_map/all_to_all | solution.py:26
  79.4 21.1 %turn_1.1 = (f32[8,256,512]{2,1,0:T(8,128)}, bf16[2048,768]{1,0:T(8,128)(2,1)S(1)}, bf16[2048,512]{1,0:T(8,128)(2,1)S(1)}, bf16[2048,512]{1,0:T(8,128)(2,1)S(1)}...) custom-call(f32[32,8,128]{2,1,0:T(8,128)S(1)} %all_to_all.70.refs_0_, ...), custom_call_target="tpu_custom_call" | custom-call | flops 25769803776 | bytes 37240832 | tf_op jit(solution)/shard_map/turn_1/pallas_call | solution.py:839
  100.4 10.0 %all_to_all.71.refs_0_ = f32[32,8,128]{2,1,0:T(8,128)S(1)} all-to-all(f32[32,8,128]{2,1,0:T(8,128)S(1)} %get-tuple-element.137), channel_id=1, replica_groups=mesh['b0'=2,'b1'=2,'b2'=2,'b3'=2,'b4'=2] {'b0','b1','b2','b3','b4'}, dimensions={0} | all-to-all | bytes 262144 | tf_op jit(solution)/shard_map/all_to_all | solution.py:26
  110.4 11.3 %adjoint_1.1 = (f32[2048,512]{1,0:T(8,128)}, f32[520,768]{1,0:T(8,128)}, f32[32,8,128]{2,1,0:T(8,128)S(1)}) custom-call(f32[32,8,128]{2,1,0:T(8,128)S(1)} %all_to_all.71.refs_0_, f32[4,2,32,8,128]{4,3,2,1,0:T(8,128)} %get-tuple-element.125.refs_1_, f32[2048,768]{1,0:T(8,128)S(1)} %get-tuple-element.138.refs_2_, f32[8,768]{1,0:T(8,128)} %get-tuple-element.139.refs_3_, ...), custom_call_target="tpu_custom_call" | custom-call | flops 12884901888 | bytes 26730496 | tf_op jit(solution)/shard_map/adjoint_1/pallas_call | solution.py:839
  122.4 167.1 %conditional.1 = (f32[2048,512]{1,0:T(8,128)}, f32[8,128]{1,0:T(8,128)}, f32[8,264,512]{2,1,0:T(8,128)}) conditional(s32[]{:T(128)} %bitcast.11, () %tuple.18, (f32[32,8,128]{2,1,0:T(8,128)S(1)}, f32[2048,512]{1,0:T(8,128)}, f32[2048,512]{1,0:T(8,128)}, f32[8,512]{1,0:T(8,128)}, bf16[2048,512]{1,0:T(8,128)(2,1)}, ...), branch_computations={%region_0.0_spmd, %region_1.6_spmd} | conditional | flops 32213606400 | bytes 115948136 | solution.py:1036
  122.5 11.2 %all_to_all.61.refs_0_ = f32[32,8,128]{2,1,0:T(8,128)S(1)} all-to-all(f32[32,8,128]{2,1,0:T(8,128)S(1)} %get-tuple-element.32), channel_id=1, replica_groups=mesh['b0'=2,'b1'=2,'b2'=2,'b3'=2,'b4'=2] {'b0','b1','b2','b3','b4'}, dimensions={0} | all-to-all | bytes 262144 | tf_op jit(solution)/shard_map/cond/branch_1_fun/all_to_all | solution.py:26
  133.6 17.4 %back_0.1 = (f32[2048,512]{1,0:T(8,128)}, bf16[2048,512]{1,0:T(8,128)(2,1)}, f32[2048,768]{1,0:T(8,128)}, f32[4,160,512]{2,1,0:T(8,128)}, f32[4,160,512]{2,1,0:T...) custom-call(f32[32,8,128]{2,1,0:T(8,128)S(1)} %all_to_all.61.refs_0_, ...), custom_call_target="tpu_custom_call" | custom-call | flops 19327352832 | bytes 36038656 | tf_op jit(solution)/shard_map/cond/branch_1_fun/back_0/pallas_call | solution.py:839
  157.7 5.2 %all-to-all-done.1.refs_0_ = f32[32,8,128]{2,1,0:T(8,128)S(1)} async-done(((f32[32,8,128]{2,1,0:T(8,128)}), f32[32,8,128]{2,1,0:T(8,128)S(1)}, u32[]{:S(2)}, u32[]{:S(2)}) %all-to-all-start.1) | async-done | bytes 131104 | tf_op jit(solution)/shard_map/cond/branch_1_fun/all_to_all | solution.py:26
  166.5 14.6 %adjoint_0.1 = (f32[8,256,512]{2,1,0:T(8,128)}, f32[8,104,512]{2,1,0:T(8,128)}) custom-call(f32[32,8,128]{2,1,0:T(8,128)S(1)} %all-to-all-done.1.refs_0_, f32[4,2,32,8,128]{4,3,2,1,0:T(8,128)} %get-tuple-element.49.refs_1_, f32[2048,768]{1,0:T(8,128)} %get-tuple-element.50.refs_2_, f32[8,768]{1,0:T(8,128)} %get-tuple-element.51.refs_3_, ...), custom_call_target="tpu_custom_call" | custom-call | flops 12884901888 | bytes 26707968 | tf_op jit(solution)/shard_map/cond/branch_1_fun/adjoint_0/pallas_call | solution.py:839
  181.1 4.0 %all-to-all-done.2 = f32[4,160,512]{2,1,0:T(8,128)S(1)} async-done(((f32[4,160,512]{2,1,0:T(8,128)}), f32[4,160,512]{2,1,0:T(8,128)S(1)}, u32[]{:S(2)}, u32[]{:S(2)}) %all-to-all-start.2) | async-done | bytes 1310752 | tf_op jit(solution)/shard_map/cond/branch_1_fun/all_to_all | solution.py:32
  185.2 6.3 %all_to_all.62 = f32[2,416,512]{2,1,0:T(8,128)S(1)} all-to-all(f32[2,416,512]{2,1,0:T(8,128)} %bitcast.17), channel_id=1, replica_groups=mesh['b0'=2,'b1'=2,'b2'=2,'b3'=2,'b4'=2] {'b4'}, dimensions={0} | all-to-all | bytes 3407872 | tf_op jit(solution)/shard_map/cond/branch_1_fun/all_to_all | solution.py:32
  196.2 13.3 %all-to-all-done.4 = f32[4,104,512]{2,1,0:T(8,128)S(1)} async-done(((f32[4,104,512]{2,1,0:T(8,128)}), f32[4,104,512]{2,1,0:T(8,128)S(1)}, u32[]{:S(2)}, u32[]{:S(2)}) %all-to-all-start.4) | async-done | bytes 852000 | tf_op jit(solution)/shard_map/cond/branch_1_fun/all_to_all | solution.py:32
  209.8 22.4 %all_to_all.63 = f32[4,72,512]{2,1,0:T(8,128)S(1)} all-to-all(f32[4,72,512]{2,1,0:T(8,128)S(1)} %bitcast.14), channel_id=1, replica_groups=mesh['b0'=2,'b1'=2,'b2'=2,'b3'=2,'b4'=2] {'b0','b1'}, dimensions={0} | all-to-all | bytes 1179648 | tf_op jit(solution)/shard_map/cond/branch_1_fun/all_to_all | solution.py:32
  232.3 21.9 %all_to_all.64 = f32[4,72,512]{2,1,0:T(8,128)S(1)} all-to-all(f32[4,72,512]{2,1,0:T(8,128)S(1)} %broadcast_in_dim.8), channel_id=1, replica_groups=mesh['b0'=2,'b1'=2,'b2'=2,'b3'=2,'b4'=2] {'b0','b1'}, dimensions={0} | all-to-all | bytes 1179648 | tf_op jit(solution)/shard_map/cond/branch_1_fun/all_to_all | solution.py:38
  254.5 26.1 %all_to_all.65 = f32[4,264,512]{2,1,0:T(8,128)S(1)} all-to-all(f32[4,264,512]{2,1,0:T(8,128)S(1)} %broadcast_in_dim.9), channel_id=1, replica_groups=mesh['b0'=2,'b1'=2,'b2'=2,'b3'=2,'b4'=2] {'b2','b3'}, dimensions={0} | all-to-all | bytes 4325376 | tf_op jit(solution)/shard_map/cond/branch_1_fun/all_to_all | solution.py:38
  281.2 8.3 %all_to_all.66 = f32[2,1056,512]{2,1,0:T(8,128)} all-to-all(f32[2,1056,512]{2,1,0:T(8,128)S(1)} %broadcast_in_dim.10), channel_id=1, replica_groups=mesh['b0'=2,'b1'=2,'b2'=2,'b3'=2,'b4'=2] {'b4'}, dimensions={0} | all-to-all | bytes 8650752 | tf_op jit(solution)/shard_map/cond/branch_1_fun/all_to_all | solution.py:38
  289.5 11.8 %last.1 = (f32[2048,512]{1,0:T(8,128)}, f32[2,512]{1,0:T(2,128)}, f32[2,512]{1,0:T(2,128)}, f32[2,384]{1,0:T(2,128)}, f32[2,384]{1,0:T(2,128)}, /*index=5*/f32[2...) custom-call(f32[8,264,512]{2,1,0:T(8,128)} %get-tuple-element.149.piece_re, ...), custom_call_target="tpu_custom_call" | custom-call | flops 1610612736 | bytes 38733824 | tf_op jit(solution)/shard_map/last/pallas_call | solution.py:839
  (23 shorter events, 19.7 us)
Async XLA Ops:
  7.2 282.3 %all-reduce.3.cloned.1.call-start = ((), (), s32[]{:S(2)}) async-start(), calls=%async_computation.14 | async-start | bytes 8470528 | tf_op jit(solution)/shard_map/psum | solution.py:1035
  121.7 0.7 copy-start
  151.0 4.0 %collective-permute-start = (f32[4,160,512]{2,1,0:T(8,128)}, f32[4,160,512]{2,1,0:T(8,128)S(1)}, u32[]{:S(2)}, u32[]{:S(2)}) collective-permute-start(f32[4,160,512]{2,1,0:T(8,128)} %get-tuple-element.47), channel_id=1, source_target_pairs={{0,1},{1,0},{2,3},{3,2},{4,5},{5,4},{6,7},{7,6},{8,9},{9,8},{10,11... | collective-permute-start | bytes 3932168 | tf_op jit(solution)/shard_map/cond/branch_1_fun/ppermute | solution.py:1015
  152.1 10.8 %all-to-all-start.1 = ((f32[32,8,128]{2,1,0:T(8,128)}), f32[32,8,128]{2,1,0:T(8,128)S(1)}, u32[]{:S(2)}, u32[]{:S(2)}) async-start(f32[32,8,128]{2,1,0:T(8,128)} %get-tuple-element.45), calls=%async_computation.1 | async-start | bytes 262144 | tf_op jit(solution)/shard_map/cond/branch_1_fun/all_to_all | solution.py:26
  162.9 22.2 %all-to-all-start.2 = ((f32[4,160,512]{2,1,0:T(8,128)}), f32[4,160,512]{2,1,0:T(8,128)S(1)}, u32[]{:S(2)}, u32[]{:S(2)}) async-start(f32[4,160,512]{2,1,0:T(8,128)} %add.6), calls=%async_computation.2 | async-start | bytes 2621440 | tf_op jit(solution)/shard_map/cond/branch_1_fun/all_to_all | solution.py:32
  192.6 16.9 %all-to-all-start.4 = ((f32[4,104,512]{2,1,0:T(8,128)}), f32[4,104,512]{2,1,0:T(8,128)S(1)}, u32[]{:S(2)}, u32[]{:S(2)}) async-start(f32[4,104,512]{2,1,0:T(8,128)} %bitcast.2), calls=%async_computation.4 | async-start | bytes 1703936 | tf_op jit(solution)/shard_map/cond/branch_1_fun/all_to_all | solution.py:32
Sparse Core Ops, SparseCore 0:
  121.9 149.7 all-reduce.2
where the time goes:
time: 309 us; the launch traced here: 308 us
  blocking collectives  151 us (49%)
  Pallas kernels  103 us (33%)
  waiting for transfers between devices  22.9 us (7%)
  between operations  14.1 us (5%)
  starting transfers between devices  10.7 us (3%)
  other arithmetic  4.17 us (1%)
    pallas_call x10, Pallas kernels, call(): pl.pallas_call(kernel, grid=(nt,), in_specs=[whole(a) if s is None else s...  103 us
    all_to_all x6, blocking collectives, gather_all(): return lax.all_to_all(copies, axes, 0, 0)  66.4 us
    all_to_all x3, blocking collectives, gather_rows(): lax.all_to_all(copies, axes, 0, 0)  56.3 us
    all_to_all x2, blocking collectives, scatter_sum(): return jnp.sum(lax.all_to_all(pieces, axes, 0, 0), axis=0)  28.7 us
    all_to_all x2, waiting for transfers between devices, scatter_sum(): return jnp.sum(lax.all_to_all(pieces, axes, 0, 0), axis=0)  17.3 us
    all_to_all x2, starting transfers between devices, scatter_sum(): return jnp.sum(lax.all_to_all(pieces, axes, 0, 0), axis=0)  7.04 us
  transfers between devices with their start and end apart: 5, of which 4 were waited for; matrix products, arithmetic and copies ran while one was open for 2% of the time, Pallas kernels for 10%

commit v1 on v0

--- a/solution.py
+++ b/solution.py
@@ -120,16 +120,18 @@
     )
 
 
-def in_stages(stages, parts):
+def in_stages(stages, parts, after={}):
     for turn in range(len(parts) + len(stages) - 1):
         for k, stage in enumerate(stages):
             if 0 <= turn - k < len(parts):
                 stage(parts[turn - k])
-
-
-def parts_of(rows, down):
-    half = rows // 2 if rows >= 32 * LANES else rows
-    parts = [(at, at + half) for at in range(0, rows, half)]
+            if turn - k == len(parts) - 1 and k in after:
+                after[k]()
+
+
+def parts_of(rows, down, count=2):
+    size = rows // count
+    parts = [(at, at + size) for at in range(0, rows, size)]
     return parts[::-1] if down else parts
 
 
@@ -361,7 +363,7 @@
         b_ref[at, :half] = re * fr - im * fi
         b_ref[at, half:] = re * fi + im * fr
 
-    in_stages([product, scan.run], parts_of(b_ref.shape[0], down))
+    in_stages([product, scan.run], parts_of(b_ref.shape[0], down, 4 if down else 2))
     scan.close()
 
     @pl.when(i == nt - 1)
@@ -490,11 +492,14 @@
             self.pg_ref[at], self.wout_ref[...], NT, preferred_element_type=F32
         )
 
-    def sums(self):
+    def gate_sum(self):
         states, width = self.wout_ref.shape
         self.wsum_ref[states : states + width] += lax.dot_general(
             self.act_ref[...], self.logit_ref[...], TN, preferred_element_type=F32
         )
+
+    def out_sum(self):
+        states = self.wout_ref.shape[0]
         self.wsum_ref[:states] += lax.dot_general(
             self.low_ref[...], self.pg_ref[...], TN, preferred_element_type=F32
         )
@@ -573,9 +578,9 @@
         live["w"], live["a"] = (wr, wi), (ar, ai)
 
     in_stages(
-        [states, mix, enter, back.middle, back.leave, weigh], parts_of(b_ref.shape[0], down)
-    )
-    back.sums()
+        [states, mix, enter, back.middle, back.leave, weigh], parts_of(b_ref.shape[0], down, 4),
+        {2: back.gate_sum, 3: back.out_sum},
+    )
     scan.close()
     put_rows(w_ref, slice(0, LANES), *live["w"])
     put_rows(ablk_ref, slice(0, LANES), *live["a"])
@@ -652,7 +657,10 @@
         else:
             res_ref[at] = result
 
-    in_stages([lambda part: scan.run(part, emit), finish], parts_of(sg_ref.shape[0], down))
+    in_stages(
+        [lambda part: scan.run(part, emit), finish],
+        parts_of(sg_ref.shape[0], down, 2 if last else 4),
+    )
     isum_ref[:width] += lax.dot_general(
         low_normed_ref[...], dg_ref[...], TN, preferred_element_type=F32
     )
@@ -728,8 +736,10 @@
         normed = (u - norm_ref[0:1]) * norm_ref[2:3] + norm_ref[3:4]
         back.enter(part, g, mixed_ref[at].astype(F32), gate_ref[at].astype(F32), normed)
 
-    in_stages([enter, back.middle, back.leave, scan.run], parts_of(sg_ref.shape[0], down))
-    back.sums()
+    in_stages(
+        [enter, back.middle, back.leave, scan.run], parts_of(sg_ref.shape[0], down),
+        {0: back.gate_sum, 1: back.out_sum},
+    )
     scan.close()
 
     @pl.when(i == nt - 1)
@@ -884,7 +894,7 @@
     steps = min(64, run)
     tile = steps * LANES
     nt = rows // tile
-    span = min(32, steps)
+    span = min(16, steps)
     def tiles(array, down):
         return (array, tile_spec(tile, array.shape[-1], nt, down))
 
@@ -918,7 +928,7 @@
     cost = rows * width * states
 
     u0_near, u0, stats = call(
-        stats_kernel, nt, [runs(tokens_run, 0), full(order)],
+        stats_kernel, nt, [near(runs(tokens_run, 0)), full(order)],
         [near(tiles(shape(rows, width, dtype=BF16), 0)), tiles(shape(rows, width, dtype=BF16), 0),
          near(full(shape(devices, 2 * SLOT, 128)))],
         [], cost // 2, "stats",

time: 309 us -> 313 us (1.013)
  no operation moved by 1% of the time
where the time goes in v1:
time: 313 us; the launch traced here: 312 us
  blocking collectives  151 us (48%)
  Pallas kernels  106 us (34%)
  waiting for transfers between devices  22.8 us (7%)
  between operations  14.1 us (5%)
  starting transfers between devices  10.7 us (3%)
  other arithmetic  4.16 us (1%)
  local copies, waits for them, and re-layouts  3.26 us (1%)
    pallas_call x10, Pallas kernels, call(): pl.pallas_call(kernel, grid=(nt,), in_specs=[whole(a) if s is None else s...  106 us
    all_to_all x6, blocking collectives, gather_all(): return lax.all_to_all(copies, axes, 0, 0)  66.5 us
    all_to_all x3, blocking collectives, gather_rows(): lax.all_to_all(copies, axes, 0, 0)  56.3 us
    all_to_all x2, blocking collectives, scatter_sum(): return jnp.sum(lax.all_to_all(pieces, axes, 0, 0), axis=0)  28.7 us
    all_to_all x2, waiting for transfers between devices, scatter_sum(): return jnp.sum(lax.all_to_all(pieces, axes, 0, 0), axis=0)  17.2 us
    all_to_all x2, starting transfers between devices, scatter_sum(): return jnp.sum(lax.all_to_all(pieces, axes, 0, 0), axis=0)  7.04 us
  transfers between devices with their start and end apart: 5, of which 4 were waited for; matrix products, arithmetic and copies ran while one was open for 2% of the time, Pallas kernels for 10%

profile of v1, /device:TPU:0, one launch (start us, length us, event | category | flops | bytes accessed | tf_op | source)
XLA Modules:
  0.0 312.3 jit_solution(18337158685708942848)
XLA Ops:
  11.6 3.8 %stats.1 = (bf16[2048,512]{1,0:T(8,128)(2,1)S(1)}, bf16[2048,512]{1,0:T(8,128)(2,1)}, f32[32,8,128]{2,1,0:T(8,128)S(1)}) custom-call(bf16[8,256,512]{2,1,0:T(8,128)(2,1)S(1)} %bitcast.13, bf16[128,128]{1,0:T(8,128)(2,1)} %get-tuple-element.119.order_ref.refs_12_), custom_call_target="tpu_custom_call" | custom-call | flops 805306368 | bytes 6455296 | tf_op jit(solution)/shard_map/stats/pallas_call | solution.py:849
  15.4 15.3 %all_to_all.67.refs_0_ = f32[32,8,128]{2,1,0:T(8,128)S(1)} all-to-all(f32[32,8,128]{2,1,0:T(8,128)S(1)} %get-tuple-element.120), channel_id=1, replica_groups=mesh['b0'=2,'b1'=2,'b2'=2,'b3'=2,'b4'=2] {'b0','b1','b2','b3','b4'}, dimensions={0} | all-to-all | bytes 262144 | tf_op jit(solution)/shard_map/all_to_all | solution.py:26
  30.7 4.9 %drive_0.1 = (f32[2048,768]{1,0:T(8,128)S(1)}, f32[32,8,128]{2,1,0:T(8,128)S(1)}, f32[8,768]{1,0:T(8,128)}, f32[8,512]{1,0:T(8,128)}) custom-call(f32[32,8,128]{2,1,0:T(8,128)S(1)} %all_to_all.67.refs_0_, bf16[2048,512]{1,0:T(8,128)(2,1)S(1)} %get-tuple-element.121.refs_1_.refs_6_, f32[2,512]{1,0:T(2,128)} %refs_2_.3, f32[2,512]{1,0:T(2,128)} %refs_3_.3, ...), custom_call_target="tpu_custom_call" | custom-call | flops 6442450944 | bytes 10334208 | tf_op jit(solution)/shard_map/drive_0/pallas_call | solution.py:849
  35.6 10.0 %all_to_all.68.refs_0_ = f32[32,8,128]{2,1,0:T(8,128)S(1)} all-to-all(f32[32,8,128]{2,1,0:T(8,128)S(1)} %get-tuple-element.124), channel_id=1, replica_groups=mesh['b0'=2,'b1'=2,'b2'=2,'b3'=2,'b4'=2] {'b0','b1','b2','b3','b4'}, dimensions={0} | all-to-all | bytes 262144 | tf_op jit(solution)/shard_map/all_to_all | solution.py:26
  45.6 9.2 %forward_0.1 = (f32[2048,512]{1,0:T(8,128)S(1)}, f32[2048,512]{1,0:T(8,128)}, bf16[2048,768]{1,0:T(8,128)(2,1)}, bf16[2048,512]{1,0:T(8,128)(2,1)}, bf16[2048,51...) custom-call(f32[32,8,128]{2,1,0:T(8,128)S(1)} %all_to_all.68.refs_0_, f32[4,2,32,8,128]{4,3,2,1,0:T(8,128)} %get-tuple-element.125.refs_1_, ...), custom_call_target="tpu_custom_call" | custom-call | flops 9663676416 | bytes 28147712 | tf_op jit(solution)/shard_map/forward_0/pallas_call | solution.py:849
  54.8 10.0 %all_to_all.69.refs_0_ = f32[32,8,128]{2,1,0:T(8,128)S(1)} all-to-all(f32[32,8,128]{2,1,0:T(8,128)S(1)} %get-tuple-element.129), channel_id=1, replica_groups=mesh['b0'=2,'b1'=2,'b2'=2,'b3'=2,'b4'=2] {'b0','b1','b2','b3','b4'}, dimensions={0} | all-to-all | bytes 262144 | tf_op jit(solution)/shard_map/all_to_all | solution.py:26
  64.8 5.0 %drive_1.1 = (f32[2048,768]{1,0:T(8,128)S(1)}, f32[32,8,128]{2,1,0:T(8,128)S(1)}, f32[8,768]{1,0:T(8,128)}, f32[8,512]{1,0:T(8,128)}) custom-call(f32[32,8,128]{2,1,0:T(8,128)S(1)} %all_to_all.69.refs_0_, f32[2048,512]{1,0:T(8,128)S(1)} %get-tuple-element.130.refs_1_, f32[2,512]{1,0:T(2,128)} %refs_2_.3, f32[2,512]{1,0:T(2,128)} %refs_3_.3, ...), custom_call_target="tpu_custom_call" | custom-call | flops 6442450944 | bytes 12431360 | tf_op jit(solution)/shard_map/drive_1/pallas_call | solution.py:849
  69.8 10.0 %all_to_all.70.refs_0_ = f32[32,8,128]{2,1,0:T(8,128)S(1)} all-to-all(f32[32,8,128]{2,1,0:T(8,128)S(1)} %get-tuple-element.131), channel_id=1, replica_groups=mesh['b0'=2,'b1'=2,'b2'=2,'b3'=2,'b4'=2] {'b0','b1','b2','b3','b4'}, dimensions={0} | all-to-all | bytes 262144 | tf_op jit(solution)/shard_map/all_to_all | solution.py:26
  79.8 24.2 %turn_1.1 = (f32[8,256,512]{2,1,0:T(8,128)}, bf16[2048,768]{1,0:T(8,128)(2,1)S(1)}, bf16[2048,512]{1,0:T(8,128)(2,1)S(1)}, bf16[2048,512]{1,0:T(8,128)(2,1)S(1)}...) custom-call(f32[32,8,128]{2,1,0:T(8,128)S(1)} %all_to_all.70.refs_0_, ...), custom_call_target="tpu_custom_call" | custom-call | flops 25769803776 | bytes 37142528 | tf_op jit(solution)/shard_map/turn_1/pallas_call | solution.py:849
  104.0 10.0 %all_to_all.71.refs_0_ = f32[32,8,128]{2,1,0:T(8,128)S(1)} all-to-all(f32[32,8,128]{2,1,0:T(8,128)S(1)} %get-tuple-element.137), channel_id=1, replica_groups=mesh['b0'=2,'b1'=2,'b2'=2,'b3'=2,'b4'=2] {'b0','b1','b2','b3','b4'}, dimensions={0} | all-to-all | bytes 262144 | tf_op jit(solution)/shard_map/all_to_all | solution.py:26
  114.0 11.4 %adjoint_1.1 = (f32[2048,512]{1,0:T(8,128)}, f32[520,768]{1,0:T(8,128)}, f32[32,8,128]{2,1,0:T(8,128)S(1)}) custom-call(f32[32,8,128]{2,1,0:T(8,128)S(1)} %all_to_all.71.refs_0_, f32[4,2,32,8,128]{4,3,2,1,0:T(8,128)} %get-tuple-element.125.refs_1_, f32[2048,768]{1,0:T(8,128)S(1)} %get-tuple-element.138.refs_2_, f32[8,768]{1,0:T(8,128)} %get-tuple-element.139.refs_3_, ...), custom_call_target="tpu_custom_call" | custom-call | flops 12884901888 | bytes 26632192 | tf_op jit(solution)/shard_map/adjoint_1/pallas_call | solution.py:849
  126.1 167.5 %conditional.1 = (f32[2048,512]{1,0:T(8,128)}, f32[8,128]{1,0:T(8,128)}, f32[8,264,512]{2,1,0:T(8,128)}) conditional(s32[]{:T(128)} %bitcast.11, () %tuple.18, (f32[32,8,128]{2,1,0:T(8,128)S(1)}, f32[2048,512]{1,0:T(8,128)}, f32[2048,512]{1,0:T(8,128)}, f32[8,512]{1,0:T(8,128)}, bf16[2048,512]{1,0:T(8,128)(2,1)}, ...), branch_computations={%region_0.0_spmd, %region_1.6_spmd} | conditional | flops 32213606400 | bytes 115849832 | solution.py:1046
  126.1 11.2 %all_to_all.61.refs_0_ = f32[32,8,128]{2,1,0:T(8,128)S(1)} all-to-all(f32[32,8,128]{2,1,0:T(8,128)S(1)} %get-tuple-element.32), channel_id=1, replica_groups=mesh['b0'=2,'b1'=2,'b2'=2,'b3'=2,'b4'=2] {'b0','b1','b2','b3','b4'}, dimensions={0} | all-to-all | bytes 262144 | tf_op jit(solution)/shard_map/cond/branch_1_fun/all_to_all | solution.py:26
  137.3 17.8 %back_0.1 = (f32[2048,512]{1,0:T(8,128)}, bf16[2048,512]{1,0:T(8,128)(2,1)}, f32[2048,768]{1,0:T(8,128)}, f32[4,160,512]{2,1,0:T(8,128)}, f32[4,160,512]{2,1,0:T...) custom-call(f32[32,8,128]{2,1,0:T(8,128)S(1)} %all_to_all.61.refs_0_, ...), custom_call_target="tpu_custom_call" | custom-call | flops 19327352832 | bytes 36038656 | tf_op jit(solution)/shard_map/cond/branch_1_fun/back_0/pallas_call | solution.py:849
  161.8 5.3 %all-to-all-done.1.refs_0_ = f32[32,8,128]{2,1,0:T(8,128)S(1)} async-done(((f32[32,8,128]{2,1,0:T(8,128)}), f32[32,8,128]{2,1,0:T(8,128)S(1)}, u32[]{:S(2)}, u32[]{:S(2)}) %all-to-all-start.1) | async-done | bytes 131104 | tf_op jit(solution)/shard_map/cond/branch_1_fun/all_to_all | solution.py:26
  170.7 14.7 %adjoint_0.1 = (f32[8,256,512]{2,1,0:T(8,128)}, f32[8,104,512]{2,1,0:T(8,128)}) custom-call(f32[32,8,128]{2,1,0:T(8,128)S(1)} %all-to-all-done.1.refs_0_, f32[4,2,32,8,128]{4,3,2,1,0:T(8,128)} %get-tuple-element.49.refs_1_, f32[2048,768]{1,0:T(8,128)} %get-tuple-element.50.refs_2_, f32[8,768]{1,0:T(8,128)} %get-tuple-element.51.refs_3_, ...), custom_call_target="tpu_custom_call" | custom-call | flops 12884901888 | bytes 26609664 | tf_op jit(solution)/shard_map/cond/branch_1_fun/adjoint_0/pallas_call | solution.py:849
  185.3 3.8 %all-to-all-done.2 = f32[4,160,512]{2,1,0:T(8,128)S(1)} async-done(((f32[4,160,512]{2,1,0:T(8,128)}), f32[4,160,512]{2,1,0:T(8,128)S(1)}, u32[]{:S(2)}, u32[]{:S(2)}) %all-to-all-start.2) | async-done | bytes 1310752 | tf_op jit(solution)/shard_map/cond/branch_1_fun/all_to_all | solution.py:32
  189.3 6.3 %all_to_all.62 = f32[2,416,512]{2,1,0:T(8,128)S(1)} all-to-all(f32[2,416,512]{2,1,0:T(8,128)} %bitcast.17), channel_id=1, replica_groups=mesh['b0'=2,'b1'=2,'b2'=2,'b3'=2,'b4'=2] {'b4'}, dimensions={0} | all-to-all | bytes 3407872 | tf_op jit(solution)/shard_map/cond/branch_1_fun/all_to_all | solution.py:32
  200.3 13.3 %all-to-all-done.4 = f32[4,104,512]{2,1,0:T(8,128)S(1)} async-done(((f32[4,104,512]{2,1,0:T(8,128)}), f32[4,104,512]{2,1,0:T(8,128)S(1)}, u32[]{:S(2)}, u32[]{:S(2)}) %all-to-all-start.4) | async-done | bytes 852000 | tf_op jit(solution)/shard_map/cond/branch_1_fun/all_to_all | solution.py:32
  213.8 22.4 %all_to_all.63 = f32[4,72,512]{2,1,0:T(8,128)S(1)} all-to-all(f32[4,72,512]{2,1,0:T(8,128)S(1)} %bitcast.15), channel_id=1, replica_groups=mesh['b0'=2,'b1'=2,'b2'=2,'b3'=2,'b4'=2] {'b0','b1'}, dimensions={0} | all-to-all | bytes 1179648 | tf_op jit(solution)/shard_map/cond/branch_1_fun/all_to_all | solution.py:32
  236.4 21.9 %all_to_all.64 = f32[4,72,512]{2,1,0:T(8,128)S(1)} all-to-all(f32[4,72,512]{2,1,0:T(8,128)S(1)} %broadcast_in_dim.8), channel_id=1, replica_groups=mesh['b0'=2,'b1'=2,'b2'=2,'b3'=2,'b4'=2] {'b0','b1'}, dimensions={0} | all-to-all | bytes 1179648 | tf_op jit(solution)/shard_map/cond/branch_1_fun/all_to_all | solution.py:38
  258.5 26.2 %all_to_all.65 = f32[4,264,512]{2,1,0:T(8,128)S(1)} all-to-all(f32[4,264,512]{2,1,0:T(8,128)S(1)} %broadcast_in_dim.9), channel_id=1, replica_groups=mesh['b0'=2,'b1'=2,'b2'=2,'b3'=2,'b4'=2] {'b2','b3'}, dimensions={0} | all-to-all | bytes 4325376 | tf_op jit(solution)/shard_map/cond/branch_1_fun/all_to_all | solution.py:38
  285.3 8.3 %all_to_all.66 = f32[2,1056,512]{2,1,0:T(8,128)} all-to-all(f32[2,1056,512]{2,1,0:T(8,128)S(1)} %broadcast_in_dim.10), channel_id=1, replica_groups=mesh['b0'=2,'b1'=2,'b2'=2,'b3'=2,'b4'=2] {'b4'}, dimensions={0} | all-to-all | bytes 8650752 | tf_op jit(solution)/shard_map/cond/branch_1_fun/all_to_all | solution.py:38
  293.6 11.8 %last.1 = (f32[2048,512]{1,0:T(8,128)}, f32[2,512]{1,0:T(2,128)}, f32[2,512]{1,0:T(2,128)}, f32[2,384]{1,0:T(2,128)}, f32[2,384]{1,0:T(2,128)}, /*index=5*/f32[2...) custom-call(f32[8,264,512]{2,1,0:T(8,128)} %get-tuple-element.149.piece_re, ...), custom_call_target="tpu_custom_call" | custom-call | flops 1610612736 | bytes 38733824 | tf_op jit(solution)/shard_map/last/pallas_call | solution.py:849
  (25 shorter events, 21.2 us)
Async XLA Ops:
  7.2 286.4 %all-reduce.3.cloned.1.call-start = ((), (), s32[]{:S(2)}) async-start(), calls=%async_computation.14 | async-start | bytes 8470528 | tf_op jit(solution)/shard_map/psum | solution.py:1045
  10.0 1.6 copy-start
  125.4 0.7 copy-start.1
  155.1 4.0 %collective-permute-start = (f32[4,160,512]{2,1,0:T(8,128)}, f32[4,160,512]{2,1,0:T(8,128)S(1)}, u32[]{:S(2)}, u32[]{:S(2)}) collective-permute-start(f32[4,160,512]{2,1,0:T(8,128)} %get-tuple-element.47), channel_id=1, source_target_pairs={{0,1},{1,0},{2,3},{3,2},{4,5},{5,4},{6,7},{7,6},{8,9},{9,8},{10,11... | collective-permute-start | bytes 3932168 | tf_op jit(solution)/shard_map/cond/branch_1_fun/ppermute | solution.py:1025
  156.2 10.9 %all-to-all-start.1 = ((f32[32,8,128]{2,1,0:T(8,128)}), f32[32,8,128]{2,1,0:T(8,128)S(1)}, u32[]{:S(2)}, u32[]{:S(2)}) async-start(f32[32,8,128]{2,1,0:T(8,128)} %get-tuple-element.45), calls=%async_computation.1 | async-start | bytes 262144 | tf_op jit(solution)/shard_map/cond/branch_1_fun/all_to_all | solution.py:26
  167.1 22.1 %all-to-all-start.2 = ((f32[4,160,512]{2,1,0:T(8,128)}), f32[4,160,512]{2,1,0:T(8,128)S(1)}, u32[]{:S(2)}, u32[]{:S(2)}) async-start(f32[4,160,512]{2,1,0:T(8,128)} %add.6), calls=%async_computation.2 | async-start | bytes 2621440 | tf_op jit(solution)/shard_map/cond/branch_1_fun/all_to_all | solution.py:32
  196.7 16.9 %all-to-all-start.4 = ((f32[4,104,512]{2,1,0:T(8,128)}), f32[4,104,512]{2,1,0:T(8,128)S(1)}, u32[]{:S(2)}, u32[]{:S(2)}) async-start(f32[4,104,512]{2,1,0:T(8,128)} %bitcast.2), calls=%async_computation.4 | async-start | bytes 1703936 | tf_op jit(solution)/shard_map/cond/branch_1_fun/all_to_all | solution.py:32
Sparse Core Ops, SparseCore 0:
  125.5 150.2 all-reduce.2

commit v2 on v0

--- a/solution.py
+++ b/solution.py
@@ -45,6 +45,43 @@
         out.append(tuple(left[-2:]))
         left = left[:-2]
     return out
+
+
+def place_in(axes):
+    place = 0
+    for axis in axes:
+        place = 2 * place + lax.axis_index(axis)
+    return place
+
+
+def traded(value, axes, mask):
+    count = 2 ** len(axes)
+    return lax.ppermute(value, axes, [(i, i ^ mask) for i in range(count)])
+
+
+def line_scatter(value, axes):
+    count = 2 ** len(axes)
+    me = place_in(axes)
+    pieces = value.reshape((count, value.shape[0] // count) + value.shape[1:])
+
+    def piece(mask):
+        return lax.dynamic_index_in_dim(pieces, me ^ mask, 0, keepdims=False)
+
+    got = [traded(piece(mask), axes, mask) for mask in range(1, count)]
+    return functools.reduce(jnp.add, got, piece(0))
+
+
+def line_gather(value, axes):
+    count = 2 ** len(axes)
+    me = place_in(axes)
+    got = [traded(value, axes, mask) for mask in range(1, count)]
+    rows = []
+    for j in range(count):
+        row = value
+        for mask in range(1, count):
+            row = jnp.where(me == j ^ mask, got[mask - 1], row)
+        rows.append(row)
+    return jnp.concatenate(rows, axis=0)
 
 
 def sum_all(value, parts):
@@ -127,9 +164,9 @@
                 stage(parts[turn - k])
 
 
-def parts_of(rows, down):
-    half = rows // 2 if rows >= 32 * LANES else rows
-    parts = [(at, at + half) for at in range(0, rows, half)]
+def parts_of(rows, down, count=2):
+    size = rows // count
+    parts = [(at, at + size) for at in range(0, rows, size)]
     return parts[::-1] if down else parts
 
 
@@ -216,7 +253,7 @@
 
 def prep_kernel(
     rows, axes, starts_ref, rate_ref, step_ref, freq_ref,
-    disc_ref, table_ref, cut_ref, order_ref,
+    disc_ref, table_ref, cut_ref,
 ):
     devices = 2 ** len(axes)
     total = rows * devices
@@ -236,12 +273,6 @@
         down = jnp.maximum(down, jnp.where((rel >= 1) & (rel <= run), rel - 1, -1))
     cut_ref[0] = up
     cut_ref[1] = down
-
-    size = order_ref.shape[0]
-    span = size // LANES
-    to = lax.broadcasted_iota(jnp.int32, (size, size), 0)
-    back = lax.broadcasted_iota(jnp.int32, (size, size), 1)
-    order_ref[...] = ((to % LANES) * span + to // LANES == back).astype(F32).astype(BF16)
 
     source = lax.broadcasted_iota(jnp.int32, (devices, half), 0)
     for l in range(LAYERS):
@@ -297,7 +328,15 @@
                 table_ref[at, 1, :, SLOT + c, :] = imag[:, cols(c)]
 
 
-def stats_kernel(tok_ref, order_ref, u_ref, copy_ref, stats_ref):
+def stats_kernel(tok_ref, u_ref, copy_ref, order_ref, stats_ref):
+    @pl.when(pl.program_id(0) == 0)
+    def _():
+        size = order_ref.shape[0]
+        span = size // LANES
+        to = lax.broadcasted_iota(jnp.int32, (size, size), 0)
+        back = lax.broadcasted_iota(jnp.int32, (size, size), 1)
+        order_ref[...] = ((to % LANES) * span + to // LANES == back).astype(F32).astype(BF16)
+
     value = permute_in(tok_ref, order_ref, (0, u_ref.shape[0]))
     u_ref[...] = value.astype(BF16)
     copy_ref[...] = u_ref[...]
@@ -361,7 +400,7 @@
         b_ref[at, :half] = re * fr - im * fi
         b_ref[at, half:] = re * fi + im * fr
 
-    in_stages([product, scan.run], parts_of(b_ref.shape[0], down))
+    in_stages([product, scan.run], parts_of(b_ref.shape[0], down, 4))
     scan.close()
 
     @pl.when(i == nt - 1)
@@ -898,13 +937,12 @@
         size = array.shape[1:]
         return (array, pl.BlockSpec((None,) + size, lambda i: (l,) + (0,) * len(size)))
 
-    discs, tables, cuts, order = call(
+    discs, tables, cuts = call(
         functools.partial(prep_kernel, rows, axes), 1,
         [full(seq_starts[None]), full(decay_rate),
          full(step_log), full(frequency)],
         [full(shape(LAYERS, 8, states)), full(shape(2 * LAYERS, 2, devices, 2 * SLOT, 128)),
-         full(shape(2, LANES, 128, dtype=jnp.int32)),
-         full(shape(span * LANES, span * LANES, dtype=BF16))],
+         full(shape(2, LANES, 128, dtype=jnp.int32))],
         [], rows * width, "prep",
     )
 
@@ -917,9 +955,10 @@
     half_scratch = [pltpu.VMEM((tile, width), BF16)] * 2
     cost = rows * width * states
 
-    u0_near, u0, stats = call(
-        stats_kernel, nt, [runs(tokens_run, 0), full(order)],
+    u0_near, u0, order, stats = call(
+        stats_kernel, nt, [runs(tokens_run, 0)],
         [near(tiles(shape(rows, width, dtype=BF16), 0)), tiles(shape(rows, width, dtype=BF16), 0),
+         full(shape(span * LANES, span * LANES, dtype=BF16)),
          near(full(shape(devices, 2 * SLOT, 128)))],
         [], cost // 2, "stats",
     )
@@ -1018,10 +1057,18 @@
         part = scatter_sum(part, chips)
         r0, in_sum0 = adjoint(0, sg0, ablk0, ends, low0, u0, norm0, pg0, g0, skip_sum0)
         in_sum0, part = lax.optimization_barrier((in_sum0, part))
-        in_part = scatter_sum(scatter_sum(in_sum0.reshape(-1, width), core), chips)
-        pad = -piece % (8 * 2 ** len(others[0]))
-        part = jnp.concatenate([part, in_part, jnp.zeros((pad, width), F32)], axis=0)
-        part = sum_all(part, others)[:piece]
+        in_part = scatter_sum(in_sum0.reshape(-1, width), core)
+        share = line_scatter(part, others[0])
+        in_part, share = lax.optimization_barrier((in_part, share))
+        in_part = scatter_sum(in_part, chips)
+        part = line_gather(share, others[0])
+        for axes_left in others[1:]:
+            part = line_gather(line_scatter(part, axes_left), axes_left)
+        in_part, part = lax.optimization_barrier((in_part, part))
+        count = in_part.shape[0]
+        pad = -count % (8 * 2 ** len(others[0]))
+        in_part = jnp.concatenate([in_part, jnp.zeros((pad, width), F32)], axis=0)
+        part = jnp.concatenate([part, sum_all(in_part, others)[:count]], axis=0)
         pieces = gather_rows(gather_rows(part, chips), core)
         return r0.reshape(rows, width), small1, pieces.reshape(BLOCKS, -1, width)
 

time: 309 us -> 303 us (0.981)
  blocking collectives: 151 us -> 126 us
  starting transfers between devices: 10.7 us -> 26.9 us
    all_to_all x6 -> x5, blocking collectives: 66.4 us -> 51.2 us  [gather_all(): return lax.all_to_all(copies, axes, 0, 0)]
    all_to_all x2, blocking collectives: 28.7 us -> 16.9 us  [scatter_sum(): return jnp.sum(lax.all_to_all(pieces, axes, 0, 0), axis=0)]
    all_to_all x2, waiting for transfers between devices: 17.3 us -> 5.69 us  [scatter_sum(): return jnp.sum(lax.all_to_all(pieces, axes, 0, 0), axis=0)]
    ppermute x0 -> x6, starting transfers between devices: none -> 8.84 us  [traded(): return lax.ppermute(value, axes, [(i, i ^ mask) for i in range(count)])]
    all_to_all x1 -> x2, starting transfers between devices: 2.57 us -> 9.87 us  [gather_all(): return lax.all_to_all(copies, axes, 0, 0)]
    ppermute x0 -> x6, waiting for transfers between devices: none -> 6.58 us  [traded(): return lax.ppermute(value, axes, [(i, i ^ mask) for i in range(count)])]
    all_to_all x1 -> x2, waiting for transfers between devices: 5.23 us -> 10.7 us  [gather_all(): return lax.all_to_all(copies, axes, 0, 0)]
  transfers between devices with their start and end apart: 5 -> 12, of which waited for: 4 -> 7; matrix products, arithmetic and copies ran while one was open for 2% -> 2% of each run, Pallas kernels for 10% -> 12%
where the time goes in v2:
time: 303 us; the launch traced here: 302 us
  blocking collectives  126 us (42%)
  Pallas kernels  103 us (34%)
  starting transfers between devices  26.9 us (9%)
  waiting for transfers between devices  23.2 us (8%)
  between operations  14.1 us (5%)
  other arithmetic  5.18 us (2%)
    pallas_call x10, Pallas kernels, call(): pl.pallas_call(kernel, grid=(nt,), in_specs=[whole(a) if s is None else s...  103 us
    all_to_all x3, blocking collectives, gather_rows(): lax.all_to_all(copies, axes, 0, 0)  58.1 us
    all_to_all x5, blocking collectives, gather_all(): return lax.all_to_all(copies, axes, 0, 0)  51.2 us
    all_to_all x2, blocking collectives, scatter_sum(): return jnp.sum(lax.all_to_all(pieces, axes, 0, 0), axis=0)  16.9 us
    all_to_all x2, waiting for transfers between devices, gather_all(): return lax.all_to_all(copies, axes, 0, 0)  10.7 us
    all_to_all x2, starting transfers between devices, gather_all(): return lax.all_to_all(copies, axes, 0, 0)  9.87 us
    ppermute x6, starting transfers between devices, traded(): return lax.ppermute(value, axes, [(i, i ^ mask) for i in range(count)])  8.84 us
    all_to_all x2, starting transfers between devices, scatter_sum(): return jnp.sum(lax.all_to_all(pieces, axes, 0, 0), axis=0)  7.06 us
  transfers between devices with their start and end apart: 12, of which 7 were waited for; matrix products, arithmetic and copies ran while one was open for 2% of the time, Pallas kernels for 12%

profile of v2, /device:TPU:0, one launch (start us, length us, event | category | flops | bytes accessed | tf_op | source)
XLA Modules:
  0.0 301.7 jit_solution(11814962879419641148)
XLA Ops:
  7.2 4.8 %stats.1 = (bf16[2048,512]{1,0:T(8,128)(2,1)S(1)}, bf16[2048,512]{1,0:T(8,128)(2,1)}, bf16[256,256]{1,0:T(8,128)(2,1)}, f32[32,8,128]{2,1,0:T(8,128)}) custom-call(bf16[8,256,512]{2,1,0:T(8,128)(2,1)} %bitcast.27), custom_call_target="tpu_custom_call" | custom-call | flops 805306368 | bytes 6553600 | tf_op jit(solution)/shard_map/stats/pallas_call | solution.py:878
  12.0 7.3 %all-to-all-start.9 = ((f32[32,8,128]{2,1,0:T(8,128)}), f32[32,8,128]{2,1,0:T(8,128)S(1)}, u32[]{:S(2)}, u32[]{:S(2)}) async-start(f32[32,8,128]{2,1,0:T(8,128)} %get-tuple-element.123), calls=%async_computation.9 | async-start | bytes 262144 | tf_op jit(solution)/shard_map/all_to_all | solution.py:26
  22.1 5.4 %all-to-all-done.9.refs_0_ = f32[32,8,128]{2,1,0:T(8,128)S(1)} async-done(((f32[32,8,128]{2,1,0:T(8,128)}), f32[32,8,128]{2,1,0:T(8,128)S(1)}, u32[]{:S(2)}, u32[]{:S(2)}) %all-to-all-start.9) | async-done | bytes 131104 | tf_op jit(solution)/shard_map/all_to_all | solution.py:26
  27.5 5.0 %drive_0.1 = (f32[2048,768]{1,0:T(8,128)S(1)}, f32[32,8,128]{2,1,0:T(8,128)S(1)}, f32[8,768]{1,0:T(8,128)}, f32[8,512]{1,0:T(8,128)}) custom-call(f32[32,8,128]{2,1,0:T(8,128)S(1)} %all-to-all-done.9.refs_0_, bf16[2048,512]{1,0:T(8,128)(2,1)S(1)} %get-tuple-element.124.refs_1_.refs_6_, f32[2,512]{1,0:T(2,128)} %refs_2_.3, f32[2,512]{1,0:T(2,128)} %refs_3_.3, ...), custom_call_target="tpu_custom_call" | custom-call | flops 6442450944 | bytes 10334208 | tf_op jit(solution)/shard_map/drive_0/pallas_call | solution.py:878
  32.5 10.0 %all_to_all.67.refs_0_ = f32[32,8,128]{2,1,0:T(8,128)S(1)} all-to-all(f32[32,8,128]{2,1,0:T(8,128)S(1)} %get-tuple-element.127), channel_id=1, replica_groups=mesh['b0'=2,'b1'=2,'b2'=2,'b3'=2,'b4'=2] {'b0','b1','b2','b3','b4'}, dimensions={0} | all-to-all | bytes 262144 | tf_op jit(solution)/shard_map/all_to_all | solution.py:26
  42.5 9.2 %forward_0.1 = (f32[2048,512]{1,0:T(8,128)S(1)}, f32[2048,512]{1,0:T(8,128)}, bf16[2048,768]{1,0:T(8,128)(2,1)}, bf16[2048,512]{1,0:T(8,128)(2,1)}, bf16[2048,51...) custom-call(f32[32,8,128]{2,1,0:T(8,128)S(1)} %all_to_all.67.refs_0_, f32[4,2,32,8,128]{4,3,2,1,0:T(8,128)} %get-tuple-element.128.refs_1_, ...), custom_call_target="tpu_custom_call" | custom-call | flops 9663676416 | bytes 28147712 | tf_op jit(solution)/shard_map/forward_0/pallas_call | solution.py:878
  51.7 10.0 %all_to_all.68.refs_0_ = f32[32,8,128]{2,1,0:T(8,128)S(1)} all-to-all(f32[32,8,128]{2,1,0:T(8,128)S(1)} %get-tuple-element.132), channel_id=1, replica_groups=mesh['b0'=2,'b1'=2,'b2'=2,'b3'=2,'b4'=2] {'b0','b1','b2','b3','b4'}, dimensions={0} | all-to-all | bytes 262144 | tf_op jit(solution)/shard_map/all_to_all | solution.py:26
  61.7 5.0 %drive_1.1 = (f32[2048,768]{1,0:T(8,128)S(1)}, f32[32,8,128]{2,1,0:T(8,128)S(1)}, f32[8,768]{1,0:T(8,128)}, f32[8,512]{1,0:T(8,128)}) custom-call(f32[32,8,128]{2,1,0:T(8,128)S(1)} %all_to_all.68.refs_0_, f32[2048,512]{1,0:T(8,128)S(1)} %get-tuple-element.133.refs_1_, f32[2,512]{1,0:T(2,128)} %refs_2_.3, f32[2,512]{1,0:T(2,128)} %refs_3_.3, ...), custom_call_target="tpu_custom_call" | custom-call | flops 6442450944 | bytes 12431360 | tf_op jit(solution)/shard_map/drive_1/pallas_call | solution.py:878
  66.7 10.0 %all_to_all.69.refs_0_ = f32[32,8,128]{2,1,0:T(8,128)S(1)} all-to-all(f32[32,8,128]{2,1,0:T(8,128)S(1)} %get-tuple-element.134), channel_id=1, replica_groups=mesh['b0'=2,'b1'=2,'b2'=2,'b3'=2,'b4'=2] {'b0','b1','b2','b3','b4'}, dimensions={0} | all-to-all | bytes 262144 | tf_op jit(solution)/shard_map/all_to_all | solution.py:26
  76.7 21.1 %turn_1.1 = (f32[8,256,512]{2,1,0:T(8,128)}, bf16[2048,768]{1,0:T(8,128)(2,1)S(1)}, bf16[2048,512]{1,0:T(8,128)(2,1)S(1)}, bf16[2048,512]{1,0:T(8,128)(2,1)S(1)}...) custom-call(f32[32,8,128]{2,1,0:T(8,128)S(1)} %all_to_all.69.refs_0_, ...), custom_call_target="tpu_custom_call" | custom-call | flops 25769803776 | bytes 37240832 | tf_op jit(solution)/shard_map/turn_1/pallas_call | solution.py:878
  97.8 10.0 %all_to_all.70.refs_0_ = f32[32,8,128]{2,1,0:T(8,128)S(1)} all-to-all(f32[32,8,128]{2,1,0:T(8,128)S(1)} %get-tuple-element.141), channel_id=1, replica_groups=mesh['b0'=2,'b1'=2,'b2'=2,'b3'=2,'b4'=2] {'b0','b1','b2','b3','b4'}, dimensions={0} | all-to-all | bytes 262144 | tf_op jit(solution)/shard_map/all_to_all | solution.py:26
  107.8 11.3 %adjoint_1.1 = (f32[2048,512]{1,0:T(8,128)}, f32[520,768]{1,0:T(8,128)}, f32[32,8,128]{2,1,0:T(8,128)S(1)}) custom-call(f32[32,8,128]{2,1,0:T(8,128)S(1)} %all_to_all.70.refs_0_, f32[4,2,32,8,128]{4,3,2,1,0:T(8,128)} %get-tuple-element.128.refs_1_, f32[2048,768]{1,0:T(8,128)S(1)} %get-tuple-element.142.refs_2_, f32[8,768]{1,0:T(8,128)} %get-tuple-element.143.refs_3_, ...), custom_call_target="tpu_custom_call" | custom-call | flops 12884901888 | bytes 26730496 | tf_op jit(solution)/shard_map/adjoint_1/pallas_call | solution.py:878
  119.9 162.6 %conditional.1 = (f32[2048,512]{1,0:T(8,128)}, f32[8,128]{1,0:T(8,128)S(1)}, f32[8,264,512]{2,1,0:T(8,128)}) conditional(s32[]{:T(128)} %bitcast.16, () %tuple.20, (f32[32,8,128]{2,1,0:T(8,128)S(1)}, f32[2048,512]{1,0:T(8,128)}, f32[2048,512]{1,0:T(8,128)}, f32[8,512]{1,0:T(8,128)}, bf16[2048,512]{1,0:T(8,128)(2,1)}, ...), branch_computations={%region_0.0_spmd, %region_1.6_spmd} | conditional | flops 32213938176 | bytes 125907784 | solution.py:1083
  119.9 11.2 %all_to_all.61.refs_0_ = f32[32,8,128]{2,1,0:T(8,128)S(1)} all-to-all(f32[32,8,128]{2,1,0:T(8,128)S(1)} %get-tuple-element.32), channel_id=1, replica_groups=mesh['b0'=2,'b1'=2,'b2'=2,'b3'=2,'b4'=2] {'b0','b1','b2','b3','b4'}, dimensions={0} | all-to-all | bytes 262144 | tf_op jit(solution)/shard_map/cond/branch_1_fun/all_to_all | solution.py:26
  131.0 17.5 %back_0.1 = (f32[2048,512]{1,0:T(8,128)}, bf16[2048,512]{1,0:T(8,128)(2,1)}, f32[2048,768]{1,0:T(8,128)}, f32[4,160,512]{2,1,0:T(8,128)}, f32[4,160,512]{2,1,0:T...) custom-call(f32[32,8,128]{2,1,0:T(8,128)S(1)} %all_to_all.61.refs_0_, ...), custom_call_target="tpu_custom_call" | custom-call | flops 19327352832 | bytes 36038656 | tf_op jit(solution)/shard_map/cond/branch_1_fun/back_0/pallas_call | solution.py:878
  155.2 5.2 %all-to-all-done.1.refs_0_ = f32[32,8,128]{2,1,0:T(8,128)S(1)} async-done(((f32[32,8,128]{2,1,0:T(8,128)}), f32[32,8,128]{2,1,0:T(8,128)S(1)}, u32[]{:S(2)}, u32[]{:S(2)}) %all-to-all-start.1) | async-done | bytes 131104 | tf_op jit(solution)/shard_map/cond/branch_1_fun/all_to_all | solution.py:26
  163.9 14.6 %adjoint_0.1 = (f32[8,256,512]{2,1,0:T(8,128)}, f32[8,104,512]{2,1,0:T(8,128)}) custom-call(f32[32,8,128]{2,1,0:T(8,128)S(1)} %all-to-all-done.1.refs_0_, f32[4,2,32,8,128]{4,3,2,1,0:T(8,128)} %get-tuple-element.49.refs_1_, f32[2048,768]{1,0:T(8,128)} %get-tuple-element.50.refs_2_, f32[8,768]{1,0:T(8,128)} %get-tuple-element.51.refs_3_, ...), custom_call_target="tpu_custom_call" | custom-call | flops 12884901888 | bytes 26707968 | tf_op jit(solution)/shard_map/cond/branch_1_fun/adjoint_0/pallas_call | solution.py:878
  183.5 4.4 %collective-permute-start.3 = (f32[40,512]{1,0:T(8,128)S(1)}, f32[40,512]{1,0:T(8,128)}, u32[]{:S(2)}, u32[]{:S(2)}) collective-permute-start(f32[40,512]{1,0:T(8,128)S(1)} %get-tuple-element.175), channel_id=1, source_target_pairs={{0,24},{8,16},{16,8},{24,0},{1,25},{9,17},{17,9},{25,1},{2,26},{10... | collective-permute-start | bytes 245768 | tf_op jit(solution)/shard_map/cond/branch_1_fun/ppermute | solution.py:59
  187.8 5.1 %all_to_all.62 = f32[2,416,512]{2,1,0:T(8,128)S(1)} all-to-all(f32[2,416,512]{2,1,0:T(8,128)S(1)} %bitcast.28), channel_id=1, replica_groups=mesh['b0'=2,'b1'=2,'b2'=2,'b3'=2,'b4'=2] {'b4'}, dimensions={0} | all-to-all | bytes 3407872 | tf_op jit(solution)/shard_map/cond/branch_1_fun/all_to_all | solution.py:32
  211.6 11.8 %all_to_all.63 = f32[4,32,512]{2,1,0:T(8,128)S(1)} all-to-all(f32[4,32,512]{2,1,0:T(8,128)S(1)} %bitcast.31), channel_id=1, replica_groups=mesh['b0'=2,'b1'=2,'b2'=2,'b3'=2,'b4'=2] {'b0','b1'}, dimensions={0} | all-to-all | bytes 524288 | tf_op jit(solution)/shard_map/cond/branch_1_fun/all_to_all | solution.py:32
  223.4 12.6 %all_to_all.64 = f32[4,32,512]{2,1,0:T(8,128)S(1)} all-to-all(f32[4,32,512]{2,1,0:T(8,128)S(1)} %broadcast_in_dim.8), channel_id=1, replica_groups=mesh['b0'=2,'b1'=2,'b2'=2,'b3'=2,'b4'=2] {'b0','b1'}, dimensions={0} | all-to-all | bytes 524288 | tf_op jit(solution)/shard_map/cond/branch_1_fun/all_to_all | solution.py:38
  236.4 37.1 %all_to_all.65 = f32[4,264,512]{2,1,0:T(8,128)S(1)} all-to-all(f32[4,264,512]{2,1,0:T(8,128)S(1)} %broadcast_in_dim.9), channel_id=1, replica_groups=mesh['b0'=2,'b1'=2,'b2'=2,'b3'=2,'b4'=2] {'b2','b3'}, dimensions={0} | all-to-all | bytes 4325376 | tf_op jit(solution)/shard_map/cond/branch_1_fun/all_to_all | solution.py:38
  274.2 8.3 %all_to_all.66 = f32[2,1056,512]{2,1,0:T(8,128)} all-to-all(f32[2,1056,512]{2,1,0:T(8,128)S(1)} %broadcast_in_dim.10), channel_id=1, replica_groups=mesh['b0'=2,'b1'=2,'b2'=2,'b3'=2,'b4'=2] {'b4'}, dimensions={0} | all-to-all | bytes 8650752 | tf_op jit(solution)/shard_map/cond/branch_1_fun/all_to_all | solution.py:38
  283.0 11.8 %last.1 = (f32[2048,512]{1,0:T(8,128)}, f32[2,512]{1,0:T(2,128)}, f32[2,512]{1,0:T(2,128)}, f32[2,384]{1,0:T(2,128)}, f32[2,384]{1,0:T(2,128)}, /*index=5*/f32[2...) custom-call(f32[8,264,512]{2,1,0:T(8,128)} %get-tuple-element.153.piece_re, ...), custom_call_target="tpu_custom_call" | custom-call | flops 1610612736 | bytes 38733824 | tf_op jit(solution)/shard_map/last/pallas_call | solution.py:878
  (47 shorter events, 38.6 us)
Async XLA Ops:
  12.0 15.5 %all-to-all-start.9 = ((f32[32,8,128]{2,1,0:T(8,128)}), f32[32,8,128]{2,1,0:T(8,128)S(1)}, u32[]{:S(2)}, u32[]{:S(2)}) async-start(f32[32,8,128]{2,1,0:T(8,128)} %get-tuple-element.123), calls=%async_computation.9 | async-start | bytes 262144 | tf_op jit(solution)/shard_map/all_to_all | solution.py:26
  19.3 263.2 %all-reduce.4.cloned.1.call-start = ((), (), s32[]{:S(2)}) async-start(), calls=%async_computation.14 | async-start | bytes 8470528 | tf_op jit(solution)/shard_map/psum | solution.py:1082
  119.2 0.7 copy-start.4
  148.5 3.9 %collective-permute-start = (f32[4,160,512]{2,1,0:T(8,128)}, f32[4,160,512]{2,1,0:T(8,128)S(1)}, u32[]{:S(2)}, u32[]{:S(2)}) collective-permute-start(f32[4,160,512]{2,1,0:T(8,128)} %get-tuple-element.47), channel_id=1, source_target_pairs={{0,1},{1,0},{2,3},{3,2},{4,5},{5,4},{6,7},{7,6},{8,9},{9,8},{10,11... | collective-permute-start | bytes 3932168 | tf_op jit(solution)/shard_map/cond/branch_1_fun/ppermute | solution.py:1054
  149.6 10.8 %all-to-all-start.1 = ((f32[32,8,128]{2,1,0:T(8,128)}), f32[32,8,128]{2,1,0:T(8,128)S(1)}, u32[]{:S(2)}, u32[]{:S(2)}) async-start(f32[32,8,128]{2,1,0:T(8,128)} %get-tuple-element.45), calls=%async_computation.1 | async-start | bytes 262144 | tf_op jit(solution)/shard_map/cond/branch_1_fun/all_to_all | solution.py:26
  160.4 22.2 %all-to-all-start.2 = ((f32[4,160,512]{2,1,0:T(8,128)}), f32[4,160,512]{2,1,0:T(8,128)S(1)}, u32[]{:S(2)}, u32[]{:S(2)}) async-start(f32[4,160,512]{2,1,0:T(8,128)} %add.26), calls=%async_computation.2 | async-start | bytes 2621440 | tf_op jit(solution)/shard_map/cond/branch_1_fun/all_to_all | solution.py:32
  178.6 9.3 %copy-start = (f32[8,104,512]{2,1,0:T(8,128)S(1)}, f32[8,104,512]{2,1,0:T(8,128)}, u32[]{:S(2)}) copy-start(f32[8,104,512]{2,1,0:T(8,128)} %get-tuple-element.61) | copy-start | bytes 5111812 | tf_op jit(solution)/shard_map/cond
  182.7 5.2 %copy-start.1 = (f32[160,512]{1,0:T(8,128)}, f32[160,512]{1,0:T(8,128)S(1)}, u32[]{:S(2)}) copy-start(f32[160,512]{1,0:T(8,128)S(1)} %reduce_sum.32) | copy-start | bytes 983044 | tf_op jit(solution)/shard_map/cond
  183.5 10.6 %collective-permute-start.1 = (f32[40,512]{1,0:T(8,128)}, f32[40,512]{1,0:T(8,128)}, u32[]{:S(2)}, u32[]{:S(2)}) collective-permute-start(f32[40,512]{1,0:T(8,128)} %get-tuple-element.174), channel_id=1, source_target_pairs={{0,8},{8,0},{16,24},{24,16},{1,9},{9,1},{17,25},{25,17},{2,10},{10... | collective-permute-start | bytes 245768 | tf_op jit(solution)/shard_map/cond/branch_1_fun/ppermute | solution.py:59
  183.5 10.6 %collective-permute-start.2 = (f32[40,512]{1,0:T(8,128)}, f32[40,512]{1,0:T(8,128)}, u32[]{:S(2)}, u32[]{:S(2)}) collective-permute-start(f32[40,512]{1,0:T(8,128)} %get-tuple-element.176), channel_id=1, source_target_pairs={{0,16},{8,24},{16,0},{24,8},{1,17},{9,25},{17,1},{25,9},{2,18},{10... | collective-permute-start | bytes 245768 | tf_op jit(solution)/shard_map/cond/branch_1_fun/ppermute | solution.py:59
  183.5 10.6 %collective-permute-start.3 = (f32[40,512]{1,0:T(8,128)S(1)}, f32[40,512]{1,0:T(8,128)}, u32[]{:S(2)}, u32[]{:S(2)}) collective-permute-start(f32[40,512]{1,0:T(8,128)S(1)} %get-tuple-element.175), channel_id=1, source_target_pairs={{0,24},{8,16},{16,8},{24,0},{1,25},{9,17},{17,9},{25,1},{2,26},{10... | collective-permute-start | bytes 245768 | tf_op jit(solution)/shard_map/cond/branch_1_fun/ppermute | solution.py:59
  195.1 16.4 %all-to-all-start.4 = ((f32[4,104,512]{2,1,0:T(8,128)}), f32[4,104,512]{2,1,0:T(8,128)S(1)}, u32[]{:S(2)}, u32[]{:S(2)}) async-start(f32[4,104,512]{2,1,0:T(8,128)} %bitcast.7), calls=%async_computation.4 | async-start | bytes 1703936 | tf_op jit(solution)/shard_map/cond/branch_1_fun/all_to_all | solution.py:32
  198.7 7.7 %collective-permute-start.4 = (f32[40,512]{1,0:T(8,128)S(1)}, f32[40,512]{1,0:T(8,128)S(1)}, u32[]{:S(2)}, u32[]{:S(2)}) collective-permute-start(f32[40,512]{1,0:T(8,128)S(1)} %fusion.1), channel_id=1, source_target_pairs={{0,24},{8,16},{16,8},{24,0},{1,25},{9,17},{17,9},{25,1},{2,26},{10... | collective-permute-start | bytes 245768 | tf_op jit(solution)/shard_map/cond/branch_1_fun/ppermute | solution.py:59
  199.4 10.3 %collective-permute-start.5 = (f32[40,512]{1,0:T(8,128)S(1)}, f32[40,512]{1,0:T(8,128)S(1)}, u32[]{:S(2)}, u32[]{:S(2)}) collective-permute-start(f32[40,512]{1,0:T(8,128)S(1)} %fusion.1), channel_id=1, source_target_pairs={{0,16},{8,24},{16,0},{24,8},{1,17},{9,25},{17,1},{25,9},{2,18},{10... | collective-permute-start | bytes 245768 | tf_op jit(solution)/shard_map/cond/branch_1_fun/ppermute | solution.py:59
  200.8 8.9 %collective-permute-start.6 = (f32[40,512]{1,0:T(8,128)S(1)}, f32[40,512]{1,0:T(8,128)S(1)}, u32[]{:S(2)}, u32[]{:S(2)}) collective-permute-start(f32[40,512]{1,0:T(8,128)S(1)} %fusion.1), channel_id=1, source_target_pairs={{0,8},{8,0},{16,24},{24,16},{1,9},{9,1},{17,25},{25,17},{2,10},{10... | collective-permute-start | bytes 245768 | tf_op jit(solution)/shard_map/cond/branch_1_fun/ppermute | solution.py:59
  274.2 8.3 %copy-start.2 = (f32[8,128]{1,0:T(8,128)S(1)}, f32[8,128]{1,0:T(8,128)}, u32[]{:S(2)}) copy-start(f32[8,128]{1,0:T(8,128)} %get-tuple-element.181) | copy-start | bytes 12292 | tf_op jit(solution)/shard_map/cond
  282.4 0.6 copy-start.3
Sparse Core Ops, SparseCore 0:
  119.3 156.6 all-reduce.3

commit v3 on v2

--- a/solution.py
+++ b/solution.py
@@ -82,14 +82,6 @@
             row = jnp.where(me == j ^ mask, got[mask - 1], row)
         rows.append(row)
     return jnp.concatenate(rows, axis=0)
-
-
-def sum_all(value, parts):
-    for part in parts:
-        value = scatter_sum(value, part)
-    for part in reversed(parts):
-        value = gather_rows(value, part)
-    return value
 
 
 def cols(c):
@@ -1068,7 +1060,9 @@
         count = in_part.shape[0]
         pad = -count % (8 * 2 ** len(others[0]))
         in_part = jnp.concatenate([in_part, jnp.zeros((pad, width), F32)], axis=0)
-        part = jnp.concatenate([part, sum_all(in_part, others)[:count]], axis=0)
+        for axes_left in others:
+            in_part = line_gather(line_scatter(in_part, axes_left), axes_left)
+        part = jnp.concatenate([part, in_part[:count]], axis=0)
         pieces = gather_rows(gather_rows(part, chips), core)
         return r0.reshape(rows, width), small1, pieces.reshape(BLOCKS, -1, width)
 

time: 303 us -> 300 us (0.990)
  blocking collectives: 126 us -> 102 us
  waiting for transfers between devices: 23.2 us -> 34.6 us
  starting transfers between devices: 26.9 us -> 35.8 us
    all_to_all x3 -> x2, blocking collectives: 58.1 us -> 45.8 us  [gather_rows(): lax.all_to_all(copies, axes, 0, 0)]
    all_to_all x2 -> x1, blocking collectives: 16.9 us -> 5.09 us  [scatter_sum(): return jnp.sum(lax.all_to_all(pieces, axes, 0, 0), axis=0)]
    ppermute x6 -> x12, waiting for transfers between devices: 6.58 us -> 18 us  [traded(): return lax.ppermute(value, axes, [(i, i ^ mask) for i in range(count)])]
    ppermute x6 -> x12, starting transfers between devices: 8.84 us -> 17.7 us  [traded(): return lax.ppermute(value, axes, [(i, i ^ mask) for i in range(count)])]
  transfers between devices with their start and end apart: 12 -> 18, of which waited for: 7 -> 11; matrix products, arithmetic and copies ran while one was open for 2% -> 2% of each run, Pallas kernels for 12% -> 12%
where the time goes in v3:
time: 300 us; the launch traced here: 299 us
  Pallas kernels  104 us (35%)
  blocking collectives  102 us (34%)
  starting transfers between devices  35.8 us (12%)
  waiting for transfers between devices  34.6 us (12%)
  between operations  14.1 us (5%)
  other arithmetic  5.25 us (2%)
    pallas_call x10, Pallas kernels, call(): pl.pallas_call(kernel, grid=(nt,), in_specs=[whole(a) if s is None else s...  104 us
    all_to_all x5, blocking collectives, gather_all(): return lax.all_to_all(copies, axes, 0, 0)  51.1 us
    all_to_all x2, blocking collectives, gather_rows(): lax.all_to_all(copies, axes, 0, 0)  45.8 us
    ppermute x12, waiting for transfers between devices, traded(): return lax.ppermute(value, axes, [(i, i ^ mask) for i in range(count)])  18 us
    ppermute x12, starting transfers between devices, traded(): return lax.ppermute(value, axes, [(i, i ^ mask) for i in range(count)])  17.7 us
    all_to_all x2, waiting for transfers between devices, gather_all(): return lax.all_to_all(copies, axes, 0, 0)  10.6 us
    all_to_all x2, starting transfers between devices, gather_all(): return lax.all_to_all(copies, axes, 0, 0)  9.86 us
    all_to_all x2, starting transfers between devices, scatter_sum(): return jnp.sum(lax.all_to_all(pieces, axes, 0, 0), axis=0)  7.06 us
  transfers between devices with their start and end apart: 18, of which 11 were waited for; matrix products, arithmetic and copies ran while one was open for 2% of the time, Pallas kernels for 12%

profile of v3, /device:TPU:0, one launch (start us, length us, event | category | flops | bytes accessed | tf_op | source)
XLA Modules:
  0.0 299.2 jit_solution(3840077848091588256)
XLA Ops:
  7.2 4.8 %stats.1 = (bf16[2048,512]{1,0:T(8,128)(2,1)S(1)}, bf16[2048,512]{1,0:T(8,128)(2,1)}, bf16[256,256]{1,0:T(8,128)(2,1)}, f32[32,8,128]{2,1,0:T(8,128)}) custom-call(bf16[8,256,512]{2,1,0:T(8,128)(2,1)} %bitcast.38), custom_call_target="tpu_custom_call" | custom-call | flops 805306368 | bytes 6553600 | tf_op jit(solution)/shard_map/stats/pallas_call | solution.py:870
  12.0 7.3 %all-to-all-start.7 = ((f32[32,8,128]{2,1,0:T(8,128)}), f32[32,8,128]{2,1,0:T(8,128)S(1)}, u32[]{:S(2)}, u32[]{:S(2)}) async-start(f32[32,8,128]{2,1,0:T(8,128)} %get-tuple-element.123), calls=%async_computation.7 | async-start | bytes 262144 | tf_op jit(solution)/shard_map/all_to_all | solution.py:26
  22.1 5.4 %all-to-all-done.7.refs_0_ = f32[32,8,128]{2,1,0:T(8,128)S(1)} async-done(((f32[32,8,128]{2,1,0:T(8,128)}), f32[32,8,128]{2,1,0:T(8,128)S(1)}, u32[]{:S(2)}, u32[]{:S(2)}) %all-to-all-start.7) | async-done | bytes 131104 | tf_op jit(solution)/shard_map/all_to_all | solution.py:26
  27.5 5.1 %drive_0.1 = (f32[2048,768]{1,0:T(8,128)S(1)}, f32[32,8,128]{2,1,0:T(8,128)S(1)}, f32[8,768]{1,0:T(8,128)}, f32[8,512]{1,0:T(8,128)}) custom-call(f32[32,8,128]{2,1,0:T(8,128)S(1)} %all-to-all-done.7.refs_0_, bf16[2048,512]{1,0:T(8,128)(2,1)S(1)} %get-tuple-element.124.refs_1_.refs_6_, f32[2,512]{1,0:T(2,128)} %refs_2_.3, f32[2,512]{1,0:T(2,128)} %refs_3_.3, ...), custom_call_target="tpu_custom_call" | custom-call | flops 6442450944 | bytes 10334208 | tf_op jit(solution)/shard_map/drive_0/pallas_call | solution.py:870
  32.6 10.0 %all_to_all.57.refs_0_ = f32[32,8,128]{2,1,0:T(8,128)S(1)} all-to-all(f32[32,8,128]{2,1,0:T(8,128)S(1)} %get-tuple-element.127), channel_id=1, replica_groups=mesh['b0'=2,'b1'=2,'b2'=2,'b3'=2,'b4'=2] {'b0','b1','b2','b3','b4'}, dimensions={0} | all-to-all | bytes 262144 | tf_op jit(solution)/shard_map/all_to_all | solution.py:26
  42.6 9.4 %forward_0.1 = (f32[2048,512]{1,0:T(8,128)S(1)}, f32[2048,512]{1,0:T(8,128)}, bf16[2048,768]{1,0:T(8,128)(2,1)}, bf16[2048,512]{1,0:T(8,128)(2,1)}, bf16[2048,51...) custom-call(f32[32,8,128]{2,1,0:T(8,128)S(1)} %all_to_all.57.refs_0_, f32[4,2,32,8,128]{4,3,2,1,0:T(8,128)} %get-tuple-element.128.refs_1_, ...), custom_call_target="tpu_custom_call" | custom-call | flops 9663676416 | bytes 28147712 | tf_op jit(solution)/shard_map/forward_0/pallas_call | solution.py:870
  52.0 10.0 %all_to_all.58.refs_0_ = f32[32,8,128]{2,1,0:T(8,128)S(1)} all-to-all(f32[32,8,128]{2,1,0:T(8,128)S(1)} %get-tuple-element.132), channel_id=1, replica_groups=mesh['b0'=2,'b1'=2,'b2'=2,'b3'=2,'b4'=2] {'b0','b1','b2','b3','b4'}, dimensions={0} | all-to-all | bytes 262144 | tf_op jit(solution)/shard_map/all_to_all | solution.py:26
  62.0 5.3 %drive_1.1 = (f32[2048,768]{1,0:T(8,128)S(1)}, f32[32,8,128]{2,1,0:T(8,128)S(1)}, f32[8,768]{1,0:T(8,128)}, f32[8,512]{1,0:T(8,128)}) custom-call(f32[32,8,128]{2,1,0:T(8,128)S(1)} %all_to_all.58.refs_0_, f32[2048,512]{1,0:T(8,128)S(1)} %get-tuple-element.133.refs_1_, f32[2,512]{1,0:T(2,128)} %refs_2_.3, f32[2,512]{1,0:T(2,128)} %refs_3_.3, ...), custom_call_target="tpu_custom_call" | custom-call | flops 6442450944 | bytes 12431360 | tf_op jit(solution)/shard_map/drive_1/pallas_call | solution.py:870
  67.2 10.0 %all_to_all.59.refs_0_ = f32[32,8,128]{2,1,0:T(8,128)S(1)} all-to-all(f32[32,8,128]{2,1,0:T(8,128)S(1)} %get-tuple-element.134), channel_id=1, replica_groups=mesh['b0'=2,'b1'=2,'b2'=2,'b3'=2,'b4'=2] {'b0','b1','b2','b3','b4'}, dimensions={0} | all-to-all | bytes 262144 | tf_op jit(solution)/shard_map/all_to_all | solution.py:26
  77.2 21.5 %turn_1.1 = (f32[8,256,512]{2,1,0:T(8,128)}, bf16[2048,768]{1,0:T(8,128)(2,1)S(1)}, bf16[2048,512]{1,0:T(8,128)(2,1)S(1)}, bf16[2048,512]{1,0:T(8,128)(2,1)S(1)}...) custom-call(f32[32,8,128]{2,1,0:T(8,128)S(1)} %all_to_all.59.refs_0_, ...), custom_call_target="tpu_custom_call" | custom-call | flops 25769803776 | bytes 37240832 | tf_op jit(solution)/shard_map/turn_1/pallas_call | solution.py:870
  98.8 10.0 %all_to_all.60.refs_0_ = f32[32,8,128]{2,1,0:T(8,128)S(1)} all-to-all(f32[32,8,128]{2,1,0:T(8,128)S(1)} %get-tuple-element.141), channel_id=1, replica_groups=mesh['b0'=2,'b1'=2,'b2'=2,'b3'=2,'b4'=2] {'b0','b1','b2','b3','b4'}, dimensions={0} | all-to-all | bytes 262144 | tf_op jit(solution)/shard_map/all_to_all | solution.py:26
  108.8 11.5 %adjoint_1.1 = (f32[2048,512]{1,0:T(8,128)}, f32[520,768]{1,0:T(8,128)}, f32[32,8,128]{2,1,0:T(8,128)S(1)}) custom-call(f32[32,8,128]{2,1,0:T(8,128)S(1)} %all_to_all.60.refs_0_, f32[4,2,32,8,128]{4,3,2,1,0:T(8,128)} %get-tuple-element.128.refs_1_, f32[2048,768]{1,0:T(8,128)S(1)} %get-tuple-element.142.refs_2_, f32[8,768]{1,0:T(8,128)} %get-tuple-element.143.refs_3_, ...), custom_call_target="tpu_custom_call" | custom-call | flops 12884901888 | bytes 26730496 | tf_op jit(solution)/shard_map/adjoint_1/pallas_call | solution.py:870
  121.0 158.9 %conditional.1 = (f32[2048,512]{1,0:T(8,128)}, f32[8,128]{1,0:T(8,128)S(1)}, f32[8,264,512]{2,1,0:T(8,128)}) conditional(s32[]{:T(128)} %bitcast.19, () %tuple.20, (f32[32,8,128]{2,1,0:T(8,128)S(1)}, f32[2048,512]{1,0:T(8,128)}, f32[2048,512]{1,0:T(8,128)}, f32[8,512]{1,0:T(8,128)}, bf16[2048,512]{1,0:T(8,128)(2,1)}, ...), branch_computations={%region_0.0_spmd, %region_1.5_spmd} | conditional | flops 32214540288 | bytes 126645336 | solution.py:1077
  121.0 11.2 %all_to_all.53.refs_0_ = f32[32,8,128]{2,1,0:T(8,128)S(1)} all-to-all(f32[32,8,128]{2,1,0:T(8,128)S(1)} %get-tuple-element.32), channel_id=1, replica_groups=mesh['b0'=2,'b1'=2,'b2'=2,'b3'=2,'b4'=2] {'b0','b1','b2','b3','b4'}, dimensions={0} | all-to-all | bytes 262144 | tf_op jit(solution)/shard_map/cond/branch_1_fun/all_to_all | solution.py:26
  132.2 17.4 %back_0.1 = (f32[2048,512]{1,0:T(8,128)}, bf16[2048,512]{1,0:T(8,128)(2,1)}, f32[2048,768]{1,0:T(8,128)}, f32[4,160,512]{2,1,0:T(8,128)}, f32[4,160,512]{2,1,0:T...) custom-call(f32[32,8,128]{2,1,0:T(8,128)S(1)} %all_to_all.53.refs_0_, ...), custom_call_target="tpu_custom_call" | custom-call | flops 19327352832 | bytes 36038656 | tf_op jit(solution)/shard_map/cond/branch_1_fun/back_0/pallas_call | solution.py:870
  156.3 5.2 %all-to-all-done.1.refs_0_ = f32[32,8,128]{2,1,0:T(8,128)S(1)} async-done(((f32[32,8,128]{2,1,0:T(8,128)}), f32[32,8,128]{2,1,0:T(8,128)S(1)}, u32[]{:S(2)}, u32[]{:S(2)}) %all-to-all-start.1) | async-done | bytes 131104 | tf_op jit(solution)/shard_map/cond/branch_1_fun/all_to_all | solution.py:26
  165.1 14.6 %adjoint_0.1 = (f32[8,256,512]{2,1,0:T(8,128)}, f32[8,104,512]{2,1,0:T(8,128)}) custom-call(f32[32,8,128]{2,1,0:T(8,128)S(1)} %all-to-all-done.1.refs_0_, f32[4,2,32,8,128]{4,3,2,1,0:T(8,128)} %get-tuple-element.49.refs_1_, f32[2048,768]{1,0:T(8,128)} %get-tuple-element.50.refs_2_, f32[8,768]{1,0:T(8,128)} %get-tuple-element.51.refs_3_, ...), custom_call_target="tpu_custom_call" | custom-call | flops 12884901888 | bytes 26707968 | tf_op jit(solution)/shard_map/cond/branch_1_fun/adjoint_0/pallas_call | solution.py:870
  179.7 4.1 %all-to-all-done.2 = f32[4,160,512]{2,1,0:T(8,128)S(1)} async-done(((f32[4,160,512]{2,1,0:T(8,128)}), f32[4,160,512]{2,1,0:T(8,128)S(1)}, u32[]{:S(2)}, u32[]{:S(2)}) %all-to-all-start.2) | async-done | bytes 1310752 | tf_op jit(solution)/shard_map/cond/branch_1_fun/all_to_all | solution.py:32
  184.7 4.4 %collective-permute-start.3 = (f32[40,512]{1,0:T(8,128)}, f32[40,512]{1,0:T(8,128)}, u32[]{:S(2)}, u32[]{:S(2)}) collective-permute-start(f32[40,512]{1,0:T(8,128)} %get-tuple-element.175), channel_id=1, source_target_pairs={{0,24},{8,16},{16,8},{24,0},{1,25},{9,17},{17,9},{25,1},{2,26},{10... | collective-permute-start | bytes 245768 | tf_op jit(solution)/shard_map/cond/branch_1_fun/ppermute | solution.py:59
  189.1 5.1 %all_to_all.54 = f32[2,416,512]{2,1,0:T(8,128)S(1)} all-to-all(f32[2,416,512]{2,1,0:T(8,128)S(1)} %bitcast.39), channel_id=1, replica_groups=mesh['b0'=2,'b1'=2,'b2'=2,'b3'=2,'b4'=2] {'b4'}, dimensions={0} | all-to-all | bytes 3407872 | tf_op jit(solution)/shard_map/cond/branch_1_fun/all_to_all | solution.py:32
  228.8 4.3 %collective-permute-done.11 = f32[32,512]{1,0:T(8,128)S(1)} collective-permute-done((f32[32,512]{1,0:T(8,128)S(1)}, f32[32,512]{1,0:T(8,128)S(1)}, u32[]{:S(2)}, u32[]{:S(2)}) %collective-permute-start.11) | collective-permute-done | bytes 65568 | tf_op jit(solution)/shard_map/cond/branch_1_fun/ppermute | solution.py:59
  233.5 37.5 %all_to_all.55 = f32[4,264,512]{2,1,0:T(8,128)S(1)} all-to-all(f32[4,264,512]{2,1,0:T(8,128)S(1)} %broadcast_in_dim.6), channel_id=1, replica_groups=mesh['b0'=2,'b1'=2,'b2'=2,'b3'=2,'b4'=2] {'b2','b3'}, dimensions={0} | all-to-all | bytes 4325376 | tf_op jit(solution)/shard_map/cond/branch_1_fun/all_to_all | solution.py:38
  271.6 8.3 %all_to_all.56 = f32[2,1056,512]{2,1,0:T(8,128)} all-to-all(f32[2,1056,512]{2,1,0:T(8,128)S(1)} %broadcast_in_dim.7), channel_id=1, replica_groups=mesh['b0'=2,'b1'=2,'b2'=2,'b3'=2,'b4'=2] {'b4'}, dimensions={0} | all-to-all | bytes 8650752 | tf_op jit(solution)/shard_map/cond/branch_1_fun/all_to_all | solution.py:38
  280.5 11.8 %last.1 = (f32[2048,512]{1,0:T(8,128)}, f32[2,512]{1,0:T(2,128)}, f32[2,512]{1,0:T(2,128)}, f32[2,384]{1,0:T(2,128)}, f32[2,384]{1,0:T(2,128)}, /*index=5*/f32[2...) custom-call(f32[8,264,512]{2,1,0:T(8,128)} %get-tuple-element.153.piece_re, ...), custom_call_target="tpu_custom_call" | custom-call | flops 1610612736 | bytes 38733824 | tf_op jit(solution)/shard_map/last/pallas_call | solution.py:870
  (57 shorter events, 50.6 us)
Async XLA Ops:
  12.0 15.5 %all-to-all-start.7 = ((f32[32,8,128]{2,1,0:T(8,128)}), f32[32,8,128]{2,1,0:T(8,128)S(1)}, u32[]{:S(2)}, u32[]{:S(2)}) async-start(f32[32,8,128]{2,1,0:T(8,128)} %get-tuple-element.123), calls=%async_computation.7 | async-start | bytes 262144 | tf_op jit(solution)/shard_map/all_to_all | solution.py:26
  19.3 260.6 %all-reduce.4.cloned.1.call-start = ((), (), s32[]{:S(2)}) async-start(), calls=%async_computation.12 | async-start | bytes 8470528 | tf_op jit(solution)/shard_map/psum | solution.py:1076
  120.3 0.7 copy-start.4
  149.6 4.0 %collective-permute-start = (f32[4,160,512]{2,1,0:T(8,128)}, f32[4,160,512]{2,1,0:T(8,128)S(1)}, u32[]{:S(2)}, u32[]{:S(2)}) collective-permute-start(f32[4,160,512]{2,1,0:T(8,128)} %get-tuple-element.47), channel_id=1, source_target_pairs={{0,1},{1,0},{2,3},{3,2},{4,5},{5,4},{6,7},{7,6},{8,9},{9,8},{10,11... | collective-permute-start | bytes 3932168 | tf_op jit(solution)/shard_map/cond/branch_1_fun/ppermute | solution.py:1046
  150.7 10.8 %all-to-all-start.1 = ((f32[32,8,128]{2,1,0:T(8,128)}), f32[32,8,128]{2,1,0:T(8,128)S(1)}, u32[]{:S(2)}, u32[]{:S(2)}) async-start(f32[32,8,128]{2,1,0:T(8,128)} %get-tuple-element.45), calls=%async_computation.1 | async-start | bytes 262144 | tf_op jit(solution)/shard_map/cond/branch_1_fun/all_to_all | solution.py:26
  161.5 22.3 %all-to-all-start.2 = ((f32[4,160,512]{2,1,0:T(8,128)}), f32[4,160,512]{2,1,0:T(8,128)S(1)}, u32[]{:S(2)}, u32[]{:S(2)}) async-start(f32[4,160,512]{2,1,0:T(8,128)} %add.39), calls=%async_computation.2 | async-start | bytes 2621440 | tf_op jit(solution)/shard_map/cond/branch_1_fun/all_to_all | solution.py:32
  179.7 9.4 %copy-start = (f32[8,104,512]{2,1,0:T(8,128)S(1)}, f32[8,104,512]{2,1,0:T(8,128)}, u32[]{:S(2)}) copy-start(f32[8,104,512]{2,1,0:T(8,128)} %get-tuple-element.61) | copy-start | bytes 5111812 | tf_op jit(solution)/shard_map/cond
  183.9 5.2 %copy-start.1 = (f32[160,512]{1,0:T(8,128)}, f32[160,512]{1,0:T(8,128)S(1)}, u32[]{:S(2)}) copy-start(f32[160,512]{1,0:T(8,128)S(1)} %reduce_sum.24) | copy-start | bytes 983044 | tf_op jit(solution)/shard_map/cond
  184.7 10.7 %collective-permute-start.1 = (f32[40,512]{1,0:T(8,128)}, f32[40,512]{1,0:T(8,128)S(1)}, u32[]{:S(2)}, u32[]{:S(2)}) collective-permute-start(f32[40,512]{1,0:T(8,128)} %get-tuple-element.174), channel_id=1, source_target_pairs={{0,8},{8,0},{16,24},{24,16},{1,9},{9,1},{17,25},{25,17},{2,10},{10... | collective-permute-start | bytes 245768 | tf_op jit(solution)/shard_map/cond/branch_1_fun/ppermute | solution.py:59
  184.7 10.7 %collective-permute-start.2 = (f32[40,512]{1,0:T(8,128)}, f32[40,512]{1,0:T(8,128)}, u32[]{:S(2)}, u32[]{:S(2)}) collective-permute-start(f32[40,512]{1,0:T(8,128)} %get-tuple-element.176), channel_id=1, source_target_pairs={{0,16},{8,24},{16,0},{24,8},{1,17},{9,25},{17,1},{25,9},{2,18},{10... | collective-permute-start | bytes 245768 | tf_op jit(solution)/shard_map/cond/branch_1_fun/ppermute | solution.py:59
  184.7 10.7 %collective-permute-start.3 = (f32[40,512]{1,0:T(8,128)}, f32[40,512]{1,0:T(8,128)}, u32[]{:S(2)}, u32[]{:S(2)}) collective-permute-start(f32[40,512]{1,0:T(8,128)} %get-tuple-element.175), channel_id=1, source_target_pairs={{0,24},{8,16},{16,8},{24,0},{1,25},{9,17},{17,9},{25,1},{2,26},{10... | collective-permute-start | bytes 245768 | tf_op jit(solution)/shard_map/cond/branch_1_fun/ppermute | solution.py:59
  196.4 16.6 %all-to-all-start.4 = ((f32[4,104,512]{2,1,0:T(8,128)}), f32[4,104,512]{2,1,0:T(8,128)S(1)}, u32[]{:S(2)}, u32[]{:S(2)}) async-start(f32[4,104,512]{2,1,0:T(8,128)} %bitcast.7), calls=%async_computation.4 | async-start | bytes 1703936 | tf_op jit(solution)/shard_map/cond/branch_1_fun/all_to_all | solution.py:32
  199.9 7.8 %collective-permute-start.4 = (f32[40,512]{1,0:T(8,128)S(1)}, f32[40,512]{1,0:T(8,128)S(1)}, u32[]{:S(2)}, u32[]{:S(2)}) collective-permute-start(f32[40,512]{1,0:T(8,128)S(1)} %fusion.2), channel_id=1, source_target_pairs={{0,24},{8,16},{16,8},{24,0},{1,25},{9,17},{17,9},{25,1},{2,26},{10... | collective-permute-start | bytes 245768 | tf_op jit(solution)/shard_map/cond/branch_1_fun/ppermute | solution.py:59
  200.8 10.4 %collective-permute-start.5 = (f32[40,512]{1,0:T(8,128)S(1)}, f32[40,512]{1,0:T(8,128)S(1)}, u32[]{:S(2)}, u32[]{:S(2)}) collective-permute-start(f32[40,512]{1,0:T(8,128)S(1)} %fusion.2), channel_id=1, source_target_pairs={{0,16},{8,24},{16,0},{24,8},{1,17},{9,25},{17,1},{25,9},{2,18},{10... | collective-permute-start | bytes 245768 | tf_op jit(solution)/shard_map/cond/branch_1_fun/ppermute | solution.py:59
  202.2 9.0 %collective-permute-start.6 = (f32[40,512]{1,0:T(8,128)S(1)}, f32[40,512]{1,0:T(8,128)S(1)}, u32[]{:S(2)}, u32[]{:S(2)}) collective-permute-start(f32[40,512]{1,0:T(8,128)S(1)} %fusion.2), channel_id=1, source_target_pairs={{0,8},{8,0},{16,24},{24,16},{1,9},{9,1},{17,25},{25,17},{2,10},{10... | collective-permute-start | bytes 245768 | tf_op jit(solution)/shard_map/cond/branch_1_fun/ppermute | solution.py:59
  213.1 5.0 %collective-permute-start.7 = (f32[32,512]{1,0:T(8,128)S(1)}, f32[32,512]{1,0:T(8,128)S(1)}, u32[]{:S(2)}, u32[]{:S(2)}) collective-permute-start(f32[32,512]{1,0:T(8,128)S(1)} %get-tuple-element.181), channel_id=1, source_target_pairs={{0,8},{8,0},{16,24},{24,16},{1,9},{9,1},{17,25},{25,17},{2,10},{10... | collective-permute-start | bytes 196616 | tf_op jit(solution)/shard_map/cond/branch_1_fun/ppermute | solution.py:59
  213.4 8.2 %collective-permute-start.8 = (f32[32,512]{1,0:T(8,128)S(1)}, f32[32,512]{1,0:T(8,128)S(1)}, u32[]{:S(2)}, u32[]{:S(2)}) collective-permute-start(f32[32,512]{1,0:T(8,128)S(1)} %get-tuple-element.183), channel_id=1, source_target_pairs={{0,16},{8,24},{16,0},{24,8},{1,17},{9,25},{17,1},{25,9},{2,18},{10... | collective-permute-start | bytes 196616 | tf_op jit(solution)/shard_map/cond/branch_1_fun/ppermute | solution.py:59
  214.1 7.5 %collective-permute-start.9 = (f32[32,512]{1,0:T(8,128)S(1)}, f32[32,512]{1,0:T(8,128)S(1)}, u32[]{:S(2)}, u32[]{:S(2)}) collective-permute-start(f32[32,512]{1,0:T(8,128)S(1)} %get-tuple-element.182), channel_id=1, source_target_pairs={{0,24},{8,16},{16,8},{24,0},{1,25},{9,17},{17,9},{25,1},{2,26},{10... | collective-permute-start | bytes 196616 | tf_op jit(solution)/shard_map/cond/branch_1_fun/ppermute | solution.py:59
  221.6 7.2 %collective-permute-start.10 = (f32[32,512]{1,0:T(8,128)S(1)}, f32[32,512]{1,0:T(8,128)S(1)}, u32[]{:S(2)}, u32[]{:S(2)}) collective-permute-start(f32[32,512]{1,0:T(8,128)S(1)} %fusion.4), channel_id=1, source_target_pairs={{0,24},{8,16},{16,8},{24,0},{1,25},{9,17},{17,9},{25,1},{2,26},{10... | collective-permute-start | bytes 196616 | tf_op jit(solution)/shard_map/cond/branch_1_fun/ppermute | solution.py:59
  223.8 9.3 %collective-permute-start.11 = (f32[32,512]{1,0:T(8,128)S(1)}, f32[32,512]{1,0:T(8,128)S(1)}, u32[]{:S(2)}, u32[]{:S(2)}) collective-permute-start(f32[32,512]{1,0:T(8,128)S(1)} %fusion.4), channel_id=1, source_target_pairs={{0,16},{8,24},{16,0},{24,8},{1,17},{9,25},{17,1},{25,9},{2,18},{10... | collective-permute-start | bytes 196616 | tf_op jit(solution)/shard_map/cond/branch_1_fun/ppermute | solution.py:59
  224.4 8.7 %collective-permute-start.12 = (f32[32,512]{1,0:T(8,128)S(1)}, f32[32,512]{1,0:T(8,128)S(1)}, u32[]{:S(2)}, u32[]{:S(2)}) collective-permute-start(f32[32,512]{1,0:T(8,128)S(1)} %fusion.4), channel_id=1, source_target_pairs={{0,8},{8,0},{16,24},{24,16},{1,9},{9,1},{17,25},{25,17},{2,10},{10... | collective-permute-start | bytes 196616 | tf_op jit(solution)/shard_map/cond/branch_1_fun/ppermute | solution.py:59
  271.6 8.3 %copy-start.2 = (f32[8,128]{1,0:T(8,128)S(1)}, f32[8,128]{1,0:T(8,128)}, u32[]{:S(2)}) copy-start(f32[8,128]{1,0:T(8,128)} %get-tuple-element.188) | copy-start | bytes 12292 | tf_op jit(solution)/shard_map/cond
  279.9 0.6 copy-start.3
Sparse Core Ops, SparseCore 0:
  120.4 155.5 all-reduce.3
